TPU v7x, 32 devices: a whole 2x2x4 slice. The times are simulated.
32 devices in a mesh: dp: 4 (over y, x), fsdp: 8 (over z, core).
Axes of the slice: x: 2, y: 2, z: 4, core: 2. Of those that a mesh axis runs over, the one named last changes fastest.
Arguments:
- tokens: bfloat16 [50176, 1024], P(('dp', 'fsdp')), may hold values from -6 to 6
- band_code: int32 [1024], P(('dp', 'fsdp')), may hold values from 0 to 3, as said below
- gsd_code: int32 [1024], P(('dp', 'fsdp')), may hold values from 0 to 6, as said below
- norm1_gain: bfloat16 [1024], P('fsdp'), may hold values from 0.5 to 1.5
- norm1_bias: bfloat16 [1024], P('fsdp'), may hold values from -1.75 to 1.75
- qkv_weight: bfloat16 [1024, 3072], P('fsdp'), may hold values from -0.25 to 0.25
- bias_q: bfloat16 [1024], P('fsdp'), may hold values from -1.75 to 1.75
- bias_v: bfloat16 [1024], P('fsdp'), may hold values from -1.75 to 1.75
- out_weight: bfloat16 [1024, 1024], P(None, 'fsdp'), may hold values from -0.5 to 0.5
- bias_out: bfloat16 [1024], P('fsdp'), may hold values from -1.75 to 1.75
- norm2_gain: bfloat16 [1024], P('fsdp'), may hold values from 0.5 to 1.5
- norm2_bias: bfloat16 [1024], P('fsdp'), may hold values from -1.75 to 1.75
- up_weight: bfloat16 [1024, 4096], P('fsdp'), may hold values from -0.1875 to 0.1875
- bias_up: bfloat16 [4096], P('fsdp'), may hold values from -1.75 to 1.75
- down_weight: bfloat16 [4096, 1024], P(None, 'fsdp'), may hold values from -0.1875 to 0.1875
- bias_down: bfloat16 [1024], P('fsdp'), may hold values from -1.75 to 1.75
- grad_out: bfloat16 [50176, 1024], P(('dp', 'fsdp')), may hold values from -6 to 6
Outputs:
- block_out: bfloat16 [50176, 1024], P(('dp', 'fsdp'))
- grad_tokens: float32 [50176, 1024], P(('dp', 'fsdp'))
- grad_norm1_gain: float32 [1024], P('fsdp')
- grad_norm1_bias: float32 [1024], P('fsdp')
- grad_qkv_weight: float32 [1024, 3072], P('fsdp')
- grad_bias_q: float32 [1024], P('fsdp')
- grad_bias_v: float32 [1024], P('fsdp')
- grad_out_weight: float32 [1024, 1024], P(None, 'fsdp')
- grad_bias_out: float32 [1024], P('fsdp')
- grad_norm2_gain: float32 [1024], P('fsdp')
- grad_norm2_bias: float32 [1024], P('fsdp')
- grad_up_weight: float32 [1024, 4096], P('fsdp')
- grad_bias_up: float32 [4096], P('fsdp')
- grad_down_weight: float32 [4096, 1024], P(None, 'fsdp')
- grad_bias_down: float32 [1024], P('fsdp')
Inputs may be any that keep to these rules, and one draw needn't show every extreme that they name: `band_code`: each device's units form 4 buffers of 8 units. A unit with code 0 is a whole RGB item; a unit with code 1 is followed in the same buffer by units with codes 2 and 3, the three band groups of one multispectral item; no item crosses a buffer. `gsd_code`: the units of one item share one level.
All inputs are finite; a program needn't handle non-finite values.
Results may differ from a plain program's by a relative error of at most 0.017.
Values may be sent and summed in bfloat16 or wider, within the bound.
A program may use at most 384 MiB of HBM per device.

v0:
```python
import math

import jax
import jax.numpy as jnp
from jax import lax
from jax.sharding import PartitionSpec as P

D = 1024
HEADS = 16
HEAD_DIM = 64
GRID = 7
UNITS_MB = 8


EPSILON = 1e-06


def layer_norm(row_block, gain_row, shift_row):
    center = row_block - jnp.mean(row_block, axis=-1, keepdims=True)
    spread = jnp.mean(center * center, axis=-1, keepdims=True)
    return center * lax.rsqrt(spread + EPSILON) * gain_row + shift_row


def gelu_exact(values):
    return 0.5 * values * (1.0 + lax.erf(values * 0.7071067811865476))


def positions(gsd_code):
    patches = GRID * GRID
    patch_place = jnp.arange(gsd_code.shape[0] * patches, dtype=jnp.int32) % patches
    across = (patch_place // GRID).astype(jnp.float32)
    along_row = (patch_place % GRID).astype(jnp.float32)
    gsd_ratio = jnp.repeat(jnp.exp2((gsd_code.astype(jnp.float32) - 3.0) * 0.5), patches)
    quarter = D // 4
    frequency = jnp.exp2(jnp.arange(quarter, dtype=jnp.float32) * (-math.log2(10000.0) / quarter))
    angle_y = (across * gsd_ratio)[:, None] * frequency[None, :]
    angle_x = (along_row * gsd_ratio)[:, None] * frequency[None, :]
    return jnp.concatenate(
        [jnp.sin(angle_y), jnp.cos(angle_y), jnp.sin(angle_x), jnp.cos(angle_x)], axis=1
    )


def item_mask(unit_codes):
    labels = jnp.cumsum((unit_codes <= 1).astype(jnp.int32))
    row_labels = jnp.repeat(labels, GRID * GRID)
    return row_labels[:, None] == row_labels[None, :]


def attention_scores(queries, keys_all, same_item):
    score_scale = 1.0 / math.sqrt(HEAD_DIM)
    scores = (
        jnp.einsum("qhe,khe->hqk", queries, keys_all, preferred_element_type=jnp.float32)
        * score_scale
    )
    return jnp.where(same_item[None], scores, -1e30)


def forward_block(gathered, token_rows, place_rows, unit_codes):
    (
        gain_one,
        shift_one,
        w_qkv,
        bias_query,
        bias_value,
        w_out,
        bias_output,
        gain_two,
        shift_two,
        w_up,
        bias_hidden,
        w_down,
        bias_final,
    ) = gathered
    row_count = token_rows.shape[0]
    model_width = w_qkv.shape[0]
    resid_in = token_rows.astype(jnp.float32) + place_rows
    normed = layer_norm(
        resid_in, gain_one.astype(jnp.float32), shift_one.astype(jnp.float32)
    ).astype(jnp.bfloat16)
    joined = jnp.concatenate([bias_query, jnp.zeros_like(bias_query), bias_value]).astype(
        jnp.float32
    )
    mixed = (jnp.dot(normed, w_qkv, preferred_element_type=jnp.float32) + joined).astype(
        jnp.bfloat16
    )
    split_heads = mixed.reshape(row_count, 3, HEADS, HEAD_DIM)
    scores = attention_scores(split_heads[:, 0], split_heads[:, 1], item_mask(unit_codes))
    row_max = jnp.max(scores, axis=-1, keepdims=True)
    log_total = row_max + jnp.log(jnp.sum(jnp.exp(scores - row_max), axis=-1, keepdims=True))
    probs = jnp.exp(scores - log_total).astype(jnp.bfloat16)
    attended = jnp.einsum(
        "hqk,khe->qhe", probs, split_heads[:, 2], preferred_element_type=jnp.float32
    )
    attended = attended.reshape(row_count, model_width).astype(jnp.bfloat16)
    middle = (
        resid_in
        + jnp.dot(attended, w_out, preferred_element_type=jnp.float32)
        + bias_output.astype(jnp.float32)
    )
    normed_two = layer_norm(
        middle, gain_two.astype(jnp.float32), shift_two.astype(jnp.float32)
    ).astype(jnp.bfloat16)
    hidden = jnp.dot(normed_two, w_up, preferred_element_type=jnp.float32) + bias_hidden.astype(
        jnp.float32
    )
    active = gelu_exact(hidden).astype(jnp.bfloat16)
    result = (
        middle
        + jnp.dot(active, w_down, preferred_element_type=jnp.float32)
        + bias_final.astype(jnp.float32)
    )
    kept_rows = (resid_in, normed, mixed, log_total, attended, middle, normed_two, hidden, active)
    return (result.astype(jnp.bfloat16), kept_rows)


def backward_block(gathered, kept_rows, grad_rows, unit_codes, totals):
    (
        gain_one,
        shift_one,
        w_qkv,
        bias_query,
        bias_value,
        w_out,
        bias_output,
        gain_two,
        shift_two,
        w_up,
        bias_hidden,
        w_down,
        bias_final,
    ) = gathered
    resid_in, normed, mixed, log_total, attended, middle, normed_two, hidden, active = kept_rows
    row_count = grad_rows.shape[0]
    model_width = w_qkv.shape[0]
    score_scale = 1.0 / math.sqrt(HEAD_DIM)
    cotangent = grad_rows.astype(jnp.float32)
    grad_down = jnp.einsum("rf,rd->fd", active, grad_rows, preferred_element_type=jnp.float32)
    grad_bias_final = jnp.sum(cotangent, axis=0)
    grad_active = jnp.einsum("rd,fd->rf", grad_rows, w_down, preferred_element_type=jnp.float32)
    gelu_value, gelu_pull = jax.vjp(gelu_exact, hidden)
    grad_hidden = gelu_pull(grad_active)[0].astype(jnp.bfloat16)
    grad_up = jnp.einsum("rd,rf->df", normed_two, grad_hidden, preferred_element_type=jnp.float32)
    grad_bias_hidden = jnp.sum(grad_hidden.astype(jnp.float32), axis=0)
    grad_normed_two = jnp.einsum("rf,df->rd", grad_hidden, w_up, preferred_element_type=jnp.float32)
    norm_value, norm_pull = jax.vjp(
        layer_norm, middle, gain_two.astype(jnp.float32), shift_two.astype(jnp.float32)
    )
    grad_middle, grad_gain_two, grad_shift_two = norm_pull(grad_normed_two)
    grad_middle = grad_middle + cotangent
    grad_branch = grad_middle.astype(jnp.bfloat16)
    grad_out_w = jnp.einsum("rd,re->de", attended, grad_branch, preferred_element_type=jnp.float32)
    grad_bias_output = jnp.sum(grad_branch.astype(jnp.float32), axis=0)
    grad_attended = jnp.einsum("re,de->rd", grad_branch, w_out, preferred_element_type=jnp.float32)
    grad_attended = grad_attended.astype(jnp.bfloat16).reshape(row_count, HEADS, HEAD_DIM)
    split_heads = mixed.reshape(row_count, 3, HEADS, HEAD_DIM)
    queries = split_heads[:, 0]
    keys_all = split_heads[:, 1]
    values_all = split_heads[:, 2]
    scores = attention_scores(queries, keys_all, item_mask(unit_codes))
    probs_full = jnp.exp(scores - log_total)
    probs = probs_full.astype(jnp.bfloat16)
    grad_values = jnp.einsum(
        "hqk,qhe->khe", probs, grad_attended, preferred_element_type=jnp.float32
    )
    grad_probs = jnp.einsum(
        "qhe,khe->hqk", grad_attended, values_all, preferred_element_type=jnp.float32
    )
    inner_sum = jnp.sum(probs_full * grad_probs, axis=-1, keepdims=True)
    grad_scores = (probs_full * (grad_probs - inner_sum)).astype(jnp.bfloat16)
    grad_queries = (
        jnp.einsum("hqk,khe->qhe", grad_scores, keys_all, preferred_element_type=jnp.float32)
        * score_scale
    )
    grad_keys = (
        jnp.einsum("hqk,qhe->khe", grad_scores, queries, preferred_element_type=jnp.float32)
        * score_scale
    )
    grad_mixed = jnp.stack([grad_queries, grad_keys, grad_values], axis=1)
    grad_mixed = grad_mixed.reshape(row_count, 3 * model_width).astype(jnp.bfloat16)
    grad_qkv = jnp.einsum("rd,rc->dc", normed, grad_mixed, preferred_element_type=jnp.float32)
    grad_mixed_f = grad_mixed.astype(jnp.float32)
    grad_bias_query = jnp.sum(grad_mixed_f[:, :model_width], axis=0)
    grad_bias_value = jnp.sum(grad_mixed_f[:, 2 * model_width :], axis=0)
    grad_normed = jnp.einsum("rc,dc->rd", grad_mixed, w_qkv, preferred_element_type=jnp.float32)
    first_value, first_pull = jax.vjp(
        layer_norm, resid_in, gain_one.astype(jnp.float32), shift_one.astype(jnp.float32)
    )
    grad_resid, grad_gain_one, grad_shift_one = first_pull(grad_normed)
    grad_token_rows = grad_resid + grad_middle
    increments = (
        grad_gain_one,
        grad_shift_one,
        grad_qkv,
        grad_bias_query,
        grad_bias_value,
        grad_out_w,
        grad_bias_output,
        grad_gain_two,
        grad_shift_two,
        grad_up,
        grad_bias_hidden,
        grad_down,
        grad_bias_final,
    )
    updated = tuple((running + extra for running, extra in zip(totals, increments)))
    return (updated, grad_token_rows)


def local(
    tokens,
    band_code,
    gsd_code,
    norm1_gain,
    norm1_bias,
    qkv_weight,
    bias_q,
    bias_v,
    out_weight,
    bias_out,
    norm2_gain,
    norm2_bias,
    up_weight,
    bias_up,
    down_weight,
    bias_down,
    grad_out,
):
    length = UNITS_MB * GRID * GRID
    gathered = (
        lax.all_gather(norm1_gain, "fsdp", axis=0, tiled=True),
        lax.all_gather(norm1_bias, "fsdp", axis=0, tiled=True),
        lax.all_gather(qkv_weight, "fsdp", axis=0, tiled=True),
        lax.all_gather(bias_q, "fsdp", axis=0, tiled=True),
        lax.all_gather(bias_v, "fsdp", axis=0, tiled=True),
        lax.all_gather(out_weight, "fsdp", axis=1, tiled=True),
        lax.all_gather(bias_out, "fsdp", axis=0, tiled=True),
        lax.all_gather(norm2_gain, "fsdp", axis=0, tiled=True),
        lax.all_gather(norm2_bias, "fsdp", axis=0, tiled=True),
        lax.all_gather(up_weight, "fsdp", axis=0, tiled=True),
        lax.all_gather(bias_up, "fsdp", axis=0, tiled=True),
        lax.all_gather(down_weight, "fsdp", axis=1, tiled=True),
        lax.all_gather(bias_down, "fsdp", axis=0, tiled=True),
    )
    token_blocks = tokens.reshape(-1, length, tokens.shape[1])
    place_blocks = positions(gsd_code).reshape(token_blocks.shape)
    code_blocks = band_code.reshape(-1, UNITS_MB)
    grad_blocks = grad_out.reshape(token_blocks.shape)
    out_blocks, kept_rows = lax.map(
        lambda pieces: forward_block(gathered, pieces[0], pieces[1], pieces[2]),
        (token_blocks, place_blocks, code_blocks),
    )
    weights_back = (
        lax.all_gather(norm1_gain, "fsdp", axis=0, tiled=True),
        lax.all_gather(norm1_bias, "fsdp", axis=0, tiled=True),
        lax.all_gather(qkv_weight, "fsdp", axis=0, tiled=True),
        lax.all_gather(bias_q, "fsdp", axis=0, tiled=True),
        lax.all_gather(bias_v, "fsdp", axis=0, tiled=True),
        lax.all_gather(out_weight, "fsdp", axis=1, tiled=True),
        lax.all_gather(bias_out, "fsdp", axis=0, tiled=True),
        lax.all_gather(norm2_gain, "fsdp", axis=0, tiled=True),
        lax.all_gather(norm2_bias, "fsdp", axis=0, tiled=True),
        lax.all_gather(up_weight, "fsdp", axis=0, tiled=True),
        lax.all_gather(bias_up, "fsdp", axis=0, tiled=True),
        lax.all_gather(down_weight, "fsdp", axis=1, tiled=True),
        lax.all_gather(bias_down, "fsdp", axis=0, tiled=True),
    )
    zero_totals = tuple((jnp.zeros(leaf.shape, jnp.float32) for leaf in weights_back))

    def backward_step(totals, pieces):
        return backward_block(weights_back, pieces[0], pieces[1], pieces[2], totals)

    totals, grad_stack = lax.scan(
        backward_step, zero_totals, (kept_rows, grad_blocks, code_blocks), reverse=True
    )
    shares = (
        lax.psum_scatter(totals[0], "fsdp", scatter_dimension=0, tiled=True),
        lax.psum_scatter(totals[1], "fsdp", scatter_dimension=0, tiled=True),
        lax.psum_scatter(totals[2], "fsdp", scatter_dimension=0, tiled=True),
        lax.psum_scatter(totals[3], "fsdp", scatter_dimension=0, tiled=True),
        lax.psum_scatter(totals[4], "fsdp", scatter_dimension=0, tiled=True),
        lax.psum_scatter(totals[5], "fsdp", scatter_dimension=1, tiled=True),
        lax.psum_scatter(totals[6], "fsdp", scatter_dimension=0, tiled=True),
        lax.psum_scatter(totals[7], "fsdp", scatter_dimension=0, tiled=True),
        lax.psum_scatter(totals[8], "fsdp", scatter_dimension=0, tiled=True),
        lax.psum_scatter(totals[9], "fsdp", scatter_dimension=0, tiled=True),
        lax.psum_scatter(totals[10], "fsdp", scatter_dimension=0, tiled=True),
        lax.psum_scatter(totals[11], "fsdp", scatter_dimension=1, tiled=True),
        lax.psum_scatter(totals[12], "fsdp", scatter_dimension=0, tiled=True),
    )
    finals = (
        lax.psum(shares[0].astype(jnp.bfloat16), "dp").astype(jnp.float32),
        lax.psum(shares[1].astype(jnp.bfloat16), "dp").astype(jnp.float32),
        lax.psum(shares[2].astype(jnp.bfloat16), "dp").astype(jnp.float32),
        lax.psum(shares[3].astype(jnp.bfloat16), "dp").astype(jnp.float32),
        lax.psum(shares[4].astype(jnp.bfloat16), "dp").astype(jnp.float32),
        lax.psum(shares[5].astype(jnp.bfloat16), "dp").astype(jnp.float32),
        lax.psum(shares[6].astype(jnp.bfloat16), "dp").astype(jnp.float32),
        lax.psum(shares[7].astype(jnp.bfloat16), "dp").astype(jnp.float32),
        lax.psum(shares[8].astype(jnp.bfloat16), "dp").astype(jnp.float32),
        lax.psum(shares[9].astype(jnp.bfloat16), "dp").astype(jnp.float32),
        lax.psum(shares[10].astype(jnp.bfloat16), "dp").astype(jnp.float32),
        lax.psum(shares[11].astype(jnp.bfloat16), "dp").astype(jnp.float32),
        lax.psum(shares[12].astype(jnp.bfloat16), "dp").astype(jnp.float32),
    )
    block_out = out_blocks.reshape(tokens.shape)
    grad_tokens = grad_stack.reshape(tokens.shape)
    return (
        block_out,
        grad_tokens,
        finals[0],
        finals[1],
        finals[2],
        finals[3],
        finals[4],
        finals[5],
        finals[6],
        finals[7],
        finals[8],
        finals[9],
        finals[10],
        finals[11],
        finals[12],
    )


def solution(mesh):
    return jax.shard_map(
        local,
        mesh=mesh,
        in_specs=(
            P(("dp", "fsdp"), None),
            P(("dp", "fsdp")),
            P(("dp", "fsdp")),
            P("fsdp"),
            P("fsdp"),
            P("fsdp", None),
            P("fsdp"),
            P("fsdp"),
            P(None, "fsdp"),
            P("fsdp"),
            P("fsdp"),
            P("fsdp"),
            P("fsdp", None),
            P("fsdp"),
            P(None, "fsdp"),
            P("fsdp"),
            P(("dp", "fsdp"), None),
        ),
        out_specs=(
            P(("dp", "fsdp"), None),
            P(("dp", "fsdp"), None),
            P("fsdp"),
            P("fsdp"),
            P("fsdp", None),
            P("fsdp"),
            P("fsdp"),
            P(None, "fsdp"),
            P("fsdp"),
            P("fsdp"),
            P("fsdp"),
            P("fsdp", None),
            P("fsdp"),
            P(None, "fsdp"),
            P("fsdp"),
        ),
        check_vma=False,
    )
```

profile of v0, /device:TPU:0, one launch (start us, length us, event | category | flops | bytes accessed | tf_op | source)
XLA Modules:
  0.0 1651.0 jit_solution(13224192189252062065)
XLA Ops:
  11.2 13.5 all-gather
  72.2 11.1 all-gather.6
  83.9 13.0 all-gather.7
  106.2 11.3 multiply_sine_fusion.1
  120.8 70.5 %all-gather.18.cloned.1.call-done = bf16[1024,4096]{1,0:T(8,128)(2,1)} async-done(((bf16[128,4096]{1,0:T(8,128)(2,1)}), bf16[1024,4096]{1,0:T(8,128)(2,1)}) %all-gather.18.cloned.1.call-update) | async-done | bytes 8388624 | tf_op jit(solution)/shard_map/all_gather | solution.py:239
  191.3 82.5 %all-gather.20.cloned.1.call-done = bf16[4096,1024]{1,0:T(8,128)(2,1)} async-done(((bf16[4096,128]{1,0:T(8,128)(2,1)}), bf16[4096,1024]{1,0:T(8,128)(2,1)}) %all-gather.20.cloned.1.call-update) | async-done | bytes 8388624 | tf_op jit(solution)/shard_map/all_gather | solution.py:241
  280.9 224.2 %while.69 = (s32[]{:T(128)}, bf16[4,392,1024]{2,1,0:T(8,128)(2,1)}, f32[4,392,1024]{2,1,0:T(8,128)}, bf16[4,392,1024]{2,1,0:T(8,128)(2,1)}, bf16[4,392,3072]{2,1...) while((s32[]{:T(128)}, bf16[4,392,1024]{2,1,0:T(8,128)(2,1)}, ...), condition=%wide.region_8.9_spmd, body=%wide.region_0.8_spmd.sunk | while | flops 10549731328 | bytes 166316816 | solution.py:248
  508.8 521.3 %while.70 = (s32[]{:T(128)}, f32[1024]{0:T(1024)S(1)}, f32[1024]{0:T(1024)S(1)}, f32[1024,3072]{1,0:T(8,128)}, f32[1024]{0:T(1024)S(1)}, /*index=5*/f32[1024]{0:...) while((s32[]{:T(128)}, f32[1024]{0:T(1024)S(1)}, ...), condition=%wide.region_29.30_spmd.clone, body=%wide.region_9.29_spmd.clone.sunk | while | flops 21401563136 | bytes 499853952 | solution.py:272
  575.6 11.6 multiply_reduce_fusion.19
  694.9 11.6 multiply_reduce_fusion.19
  746.9 13.2 select_add_fusion.33
  760.1 12.7 select_add_fusion.35
  821.5 11.6 multiply_reduce_fusion.19
  873.5 13.2 select_add_fusion.33
  886.7 12.7 select_add_fusion.35
  948.1 11.6 multiply_reduce_fusion.19
  1000.1 13.2 select_add_fusion.33
  1013.2 12.7 select_add_fusion.35
  1032.3 46.2 %reduce-scatter.7.cloned.1.call-done = f32[1024,128]{1,0:T(8,128)} async-done(((f32[1024,1024]{1,0:T(8,128)}), f32[1024,128]{1,0:T(8,128)}) %reduce-scatter.7.cloned.1.call-update) | async-done | bytes 524304 | tf_op jit(solution)/shard_map/reduce_scatter | solution.py:281
  1080.3 127.8 %reduce-scatter.5.cloned.1.call-done = f32[128,3072]{1,0:T(8,128)} async-done(((f32[1024,3072]{1,0:T(8,128)}), f32[128,3072]{1,0:T(8,128)}) %reduce-scatter.5.cloned.1.call-update) | async-done | bytes 1572880 | tf_op jit(solution)/shard_map/reduce_scatter | solution.py:278
  1210.4 166.6 %reduce-scatter.9.cloned.1.call-done = f32[128,4096]{1,0:T(8,128)} async-done(((f32[1024,4096]{1,0:T(8,128)}), f32[128,4096]{1,0:T(8,128)}) %reduce-scatter.9.cloned.1.call-update) | async-done | bytes 2097168 | tf_op jit(solution)/shard_map/reduce_scatter | solution.py:285
  1379.7 166.3 %reduce-scatter.11.cloned.1.call-done = f32[4096,128]{1,0:T(8,128)} async-done(((f32[4096,1024]{1,0:T(8,128)}), f32[4096,128]{1,0:T(8,128)}) %reduce-scatter.11.cloned.1.call-update) | async-done | bytes 2097168 | tf_op jit(solution)/shard_map/reduce_scatter | solution.py:287
  1550.6 26.4 %all-reduce.9 = (bf16[1024]{0:T(1024)(128)(2,1)S(1)}, bf16[1024]{0:T(1024)(128)(2,1)S(1)}, bf16[1024]{0:T(1024)(128)(2,1)S(1)}, bf16[1024]{0:T(1024)(128)(2,1)S(...) all-reduce(f32[1024]{0:T(1024)S(1)} %get-tuple-element.1934, ...), channel_id=2, replica_groups=mesh['dp'=4,'fsdp'=8] {'fsdp'}, use_global_device_ids=true, to_apply=%region_30.31.clone | all-reduce | flops 12288 | bytes 73728
  1592.8 43.9 %all-reduce.14.cloned.1.call-done = (bf16[128,3072]{1,0:T(8,128)(2,1)}, bf16[1024,128]{1,0:T(8,128)(2,1)}, bf16[128,4096]{1,0:T(8,128)(2,1)}, bf16[4096,128]{1,0:T(8,128)(2,1)}) async-done(((bf16[128,3072]{1,0:T(8,128)(2,1)}, bf16[1024,128]{1,0:T(8,128)(2,1)}, bf16[128,4096]{1,0:T(8,128)(2,1)}, bf16[4096,128]{1,0:T(8,128)(2,1)}), (bf16[128,3072]{1,0:T(8,128)(2,1)}, bf16[1024,128]{1,0:T(8,128)(2,1)}, ...) | async-done | bytes 3145744 | tf_op jit(solution)/shard_map/psum | solution.py:293
  (729 shorter events, 706.8 us)
Async XLA Ops:
  7.2 26.3 %copy-start.34 = (bf16[128]{0:T(256)(128)(2,1)S(1)}, bf16[128]{0:T(256)(128)(2,1)}, u32[]{:S(2)}) copy-start(bf16[128]{0:T(256)(128)(2,1)} %param.27) | copy-start | bytes 772
  7.2 36.4 %copy-start.35 = (bf16[128]{0:T(256)(128)(2,1)S(1)}, bf16[128]{0:T(256)(128)(2,1)}, u32[]{:S(2)}) copy-start(bf16[128]{0:T(256)(128)(2,1)} %param.28) | copy-start | bytes 772
  7.2 45.1 %copy-start.36 = (s32[32]{0:T(128)S(1)}, s32[32]{0:T(128)}, u32[]{:S(2)}) copy-start(s32[32]{0:T(128)} %param.22) | copy-start | bytes 388
  7.2 45.7 %copy-start.37 = (bf16[128]{0:T(256)(128)(2,1)S(1)}, bf16[128]{0:T(256)(128)(2,1)}, u32[]{:S(2)}) copy-start(bf16[128]{0:T(256)(128)(2,1)} %param.30) | copy-start | bytes 772
  7.2 56.2 %copy-start.38 = (bf16[128]{0:T(256)(128)(2,1)S(1)}, bf16[128]{0:T(256)(128)(2,1)}, u32[]{:S(2)}) copy-start(bf16[128]{0:T(256)(128)(2,1)} %param.31) | copy-start | bytes 772
  7.3 64.9 %copy-start.39 = (bf16[128]{0:T(256)(128)(2,1)S(1)}, bf16[128]{0:T(256)(128)(2,1)}, u32[]{:S(2)}) copy-start(bf16[128]{0:T(256)(128)(2,1)} %param.32) | copy-start | bytes 772
  7.3 76.6 %copy-start.31 = (bf16[512]{0:T(512)(128)(2,1)S(1)}, bf16[512]{0:T(512)(128)(2,1)}, u32[]{:S(2)}) copy-start(bf16[512]{0:T(512)(128)(2,1)} %param.34) | copy-start | bytes 3076
  7.3 89.6 %copy-start.40 = (bf16[128]{0:T(256)(128)(2,1)S(1)}, bf16[128]{0:T(256)(128)(2,1)}, u32[]{:S(2)}) copy-start(bf16[128]{0:T(256)(128)(2,1)} %param.36) | copy-start | bytes 772
  7.3 113.5 %all-gather.16.cloned.1.call-start = ((), (), s32[]{:S(2)}) async-start(), calls=%async_computation.5 | async-start | bytes 2359296 | tf_op jit(solution)/shard_map/all_gather | solution.py:235
  8.0 112.8 %all-gather.14.cloned.1.call-start = ((), (), s32[]{:S(2)}) async-start(), calls=%async_computation.4 | async-start | bytes 7077888 | tf_op jit(solution)/shard_map/all_gather | solution.py:232
  8.8 182.6 %all-gather.18.cloned.1.call-start = ((), (), s32[]{:S(2)}) async-start(), calls=%async_computation.6 | async-start | bytes 9437184 | tf_op jit(solution)/shard_map/all_gather | solution.py:239
  9.5 264.3 %all-gather.20.cloned.1.call-start = ((), (), s32[]{:S(2)}) async-start(), calls=%async_computation.7 | async-start | bytes 9437184 | tf_op jit(solution)/shard_map/all_gather | solution.py:241
  10.1 1068.4 %reduce-scatter.7.cloned.1.call-start = ((), (), s32[]{:S(2)}) async-start(), calls=%async_computation.9 | async-start | bytes 4718592 | tf_op jit(solution)/shard_map/reduce_scatter | solution.py:281
  575.5 18.8 %slice-start = ((s8[12845056]{0:T(1024)(128)(4,1)}), s8[4194304]{0:T(1024)(128)(4,1)S(1)}, s32[]{:S(2)}) async-start(s8[12845056]{0:T(1024)(128)(4,1)} %bitcast.319), calls=%async_computation.13 | async-start | bytes 8388608 | tf_op jit(solution)/shard_map/while
  575.5 18.8 %slice-start.1 = ((s8[12845056]{0:T(1024)(128)(4,1)}), s8[4194304]{0:T(1024)(128)(4,1)S(1)}, s32[]{:S(2)}) async-start(s8[12845056]{0:T(1024)(128)(4,1)} %bitcast.319), calls=%async_computation.14 | async-start | bytes 8388608 | tf_op jit(solution)/shard_map/while
  694.9 18.8 %slice-start = ((s8[12845056]{0:T(1024)(128)(4,1)}), s8[4194304]{0:T(1024)(128)(4,1)S(1)}, s32[]{:S(2)}) async-start(s8[12845056]{0:T(1024)(128)(4,1)} %bitcast.319), calls=%async_computation.13 | async-start | bytes 8388608 | tf_op jit(solution)/shard_map/while
  694.9 18.8 %slice-start.1 = ((s8[12845056]{0:T(1024)(128)(4,1)}), s8[4194304]{0:T(1024)(128)(4,1)S(1)}, s32[]{:S(2)}) async-start(s8[12845056]{0:T(1024)(128)(4,1)} %bitcast.319), calls=%async_computation.14 | async-start | bytes 8388608 | tf_op jit(solution)/shard_map/while
  821.5 18.8 %slice-start = ((s8[12845056]{0:T(1024)(128)(4,1)}), s8[4194304]{0:T(1024)(128)(4,1)S(1)}, s32[]{:S(2)}) async-start(s8[12845056]{0:T(1024)(128)(4,1)} %bitcast.319), calls=%async_computation.13 | async-start | bytes 8388608 | tf_op jit(solution)/shard_map/while
  948.0 18.8 %slice-start = ((s8[12845056]{0:T(1024)(128)(4,1)}), s8[4194304]{0:T(1024)(128)(4,1)S(1)}, s32[]{:S(2)}) async-start(s8[12845056]{0:T(1024)(128)(4,1)} %bitcast.319), calls=%async_computation.13 | async-start | bytes 8388608 | tf_op jit(solution)/shard_map/while
  1030.2 177.9 %reduce-scatter.5.cloned.1.call-start = ((), (), s32[]{:S(2)}) async-start(), calls=%async_computation.8 | async-start | bytes 14155776 | tf_op jit(solution)/shard_map/reduce_scatter | solution.py:278
  1030.7 346.3 %reduce-scatter.9.cloned.1.call-start = ((), (), s32[]{:S(2)}) async-start(), calls=%async_computation.10 | async-start | bytes 18874368 | tf_op jit(solution)/shard_map/reduce_scatter | solution.py:285
  1031.5 514.6 %reduce-scatter.11.cloned.1.call-start = ((), (), s32[]{:S(2)}) async-start(), calls=%async_computation.11 | async-start | bytes 18874368 | tf_op jit(solution)/shard_map/reduce_scatter | solution.py:287
  1032.2 604.5 %all-reduce.14.cloned.1.call-start = ((), (), s32[]{:S(2)}) async-start(), calls=%async_computation.12 | async-start | bytes 6291456 | tf_op jit(solution)/shard_map/psum | solution.py:293
  1379.7 169.0 %copy-start.41 = (u32[32]{0:T(128)S(1)}, u32[32]{0:T(128)}, u32[]{:S(2)}) copy-start(u32[32]{0:T(128)} %constant.261) | copy-start | bytes 388
  (124 other events, 798.1 us)
Sparse Core Ops, SparseCore 0:
  9.7 33.5 all-gather.15
  45.0 64.0 all-gather.13
  110.6 80.6 all-gather.17
  192.8 81.0 all-gather.19
  1030.3 48.1 reduce-scatter.6
  1080.7 127.3 reduce-scatter.4
  1210.4 166.5 reduce-scatter.8
  1379.4 166.6 reduce-scatter.10
  1550.6 86.1 all-reduce.13
where the time goes:
time: 1660 us; the launch traced here: 1650 us
  waiting for transfers between devices  708 us (43%)
  matrix products  488 us (29%)
  other arithmetic  188 us (11%)
  blocking collectives  130 us (8%)
  local copies, waits for them, and re-layouts  95.7 us (6%)
  loops' own time  25.1 us (2%)
    reduce_scatter x1, waiting for transfers between devices, local(): lax.psum_scatter(totals[9], 'fsdp', scatter_dimension=0, tiled=True)  167 us
    reduce_scatter x1, waiting for transfers between devices, local(): lax.psum_scatter(totals[11], 'fsdp', scatter_dimension=1, tiled=True)  166 us
    reduce_scatter x1, waiting for transfers between devices, local(): lax.psum_scatter(totals[2], 'fsdp', scatter_dimension=0, tiled=True)  128 us
    all_gather x1, waiting for transfers between devices, local(): lax.all_gather(down_weight, 'fsdp', axis=1, tiled=True)  82.5 us
    all_gather x1, waiting for transfers between devices, local(): lax.all_gather(up_weight, 'fsdp', axis=0, tiled=True)  70.5 us
    dot_general x8, matrix products, attention_scores(): jnp.einsum('qhe,khe->hqk', queries, keys_all, preferred_element_type=jnp....  62 us
    dynamic_update_slice x20, other arithmetic, local(): lax.map(lambda pieces: forward_block(gathered, pieces[0], pieces[1], piec...  51.8 us
    dot_general x4, matrix products, backward_block(): jnp.einsum('rd,rf->df', normed_two, grad_hidden, preferred_element_type=j...  49.6 us
  transfers between devices with their start and end apart: 9, of which 7 were waited for; matrix products, arithmetic and copies ran while one was open for 2% of the time, Pallas kernels for 0%

commit v1 on v0

v1 whole, which is shorter than its diff:
```python
import functools
import math

import jax
import jax.numpy as jnp
import numpy as np
from jax import lax
from jax.experimental import pallas as pl
from jax.experimental.pallas import tpu as pltpu
from jax.sharding import PartitionSpec as P

bf = jnp.bfloat16
f32 = jnp.float32
NN = (((1,), (0,)), ((), ()))
NT = (((1,), (1,)), ((), ()))
TN = (((0,), (0,)), ((), ()))
D = 1024
HEADS = 16
HEAD_DIM = 64
GRID = 7
UNIT = GRID * GRID
UNITS_MB = 8
BUF = UNIT * UNITS_MB
PAIR = 2 * BUF
QUADS = 4
QW = 256
FC = 512
CW = 1024
EPS = 1e-6
SCALE = 0.125
NEG = -1e30
VMEM_LIMIT = 60 << 20
KEYS = 384
WINDOWS = ((0, ((0, 192, 0), (192, 208, 16))), (384, ((0, 192, 0), (192, 208, 16))))
QMAX = 208


def dot(a, b, dims=NN):
    return lax.dot_general(a, b, dims, preferred_element_type=f32)


def any_spec():
    return pl.BlockSpec(memory_space=pl.ANY)


def vmem_spec():
    return pl.BlockSpec(memory_space=pltpu.VMEM)


def sds(shape, kind):
    return jax.ShapeDtypeStruct(shape, kind)


def norm_parts(v):
    center = v - jnp.mean(v, axis=-1, keepdims=True)
    inv = lax.rsqrt(jnp.mean(center * center, axis=-1, keepdims=True) + EPS)
    return center * inv, inv


def transpose_rows(src, dst, rows):
    full = rows // 128

    def one(i, carry):
        o = pl.multiple_of(i * 128, 128)
        dst[:, pl.ds(o, 128)] = src[pl.ds(o, 128), :].T
        return carry

    lax.fori_loop(0, full, one, 0)
    if rows % 128:
        dst[:, full * 128 : rows] = src[full * 128 : rows, :].T


def fill_bias(bias, lab_col, lab_row, q_units, k_units):
    same = jnp.where(lab_col[...] == lab_row[...], 1.0, 0.0).astype(bf)

    def one(i, carry):
        reach = dot(q_units[i], same).astype(bf)
        bias[i] = (dot(reach, k_units[i]) - 1.0) * -NEG
        return carry

    lax.fori_loop(0, bias.shape[0], one, 0)


def half_mask(rows, second):
    lane = lax.broadcasted_iota(jnp.int32, (rows, 128), 1)
    return lane >= 64 if second else lane < 64


def attention_forward(pairs, mixed, bias, attended, lse, quad, hook):
    def one(i, carry):
        p, hp = i // 2, lax.rem(i, 2)
        base = pl.multiple_of(p * PAIR, 16)
        lane0 = pl.multiple_of(hp * 128, 128)
        tail = None
        for w, (start, halves) in enumerate(WINDOWS):
            for n, (q0, qn, k0) in enumerate(halves):
                row = pl.multiple_of(base + start + q0, 16)
                keys = pl.ds(pl.multiple_of(base + start + k0, 16), KEYS)
                q2 = mixed[pl.ds(row, qn), pl.ds(lane0, 128)] * jnp.asarray(SCALE, bf)
                k2 = mixed[keys, pl.ds(pl.multiple_of(lane0 + QW, 128), 128)]
                v2 = mixed[keys, pl.ds(pl.multiple_of(lane0 + 2 * QW, 128), 128)]
                idx = p * 4 + w * 2 + n
                out = None
                lse_new = jnp.zeros((qn, 128), f32)
                lane = lax.broadcasted_iota(jnp.int32, (qn, 128), 1)
                for h in range(2):
                    qm = jnp.where(half_mask(qn, h == 1), q2, jnp.zeros_like(q2))
                    s = dot(qm, k2, NT) + bias[idx, 0:qn, :]
                    m = jnp.max(s, axis=-1, keepdims=True)
                    e = jnp.exp(s - m)
                    total = jnp.sum(e, axis=-1, keepdims=True)
                    probs = (e * (1.0 / total)).astype(bf)
                    o = dot(probs, v2)
                    out = o if h == 0 else jnp.where(half_mask(qn, True), o, out)
                    head = quad * 4 + hp * 2 + h
                    lse_new = jnp.where(lane == head, m + jnp.log(total), lse_new)
                if w == 0 and n == 1:
                    tail = (out[qn - 16 :], lse_new[qn - 16 :])
                if w == 1 and n == 0:
                    first = lax.broadcasted_iota(jnp.int32, (16, 128), 0) < 8
                    out = jnp.concatenate([jnp.where(first, tail[0], out[0:16]), out[16:]], axis=0)
                    lse_new = jnp.concatenate([jnp.where(first, tail[1], lse_new[0:16]), lse_new[16:]], axis=0)
                attended[pl.ds(row, qn), pl.ds(lane0, 128)] = out.astype(bf)
                head0 = quad * 4 + hp * 2
                keep = (lane == head0) | (lane == head0 + 1)
                lse[pl.ds(row, qn), :] = jnp.where(keep, lse_new, lse[pl.ds(row, qn), :])
        hook(i)
        return carry

    lax.fori_loop(0, pairs * 2, one, 0)


MESH = pl.DeviceIdType.MESH


class Place:
    def __init__(self):
        self.d = lax.axis_index("dp")
        self.f = lax.axis_index("fsdp")
        self.z = lax.div(self.f, 2)
        self.c = lax.rem(self.f, 2)
        self.dx = self.d + 1 - 2 * lax.rem(self.d, 2)
        self.dy = lax.rem(self.d + 2, 4)
        self.dd = 3 - self.d
        self.sib = self.f + 1 - 2 * self.c
        self.zs = [lax.rem(self.z + n, 4) for n in (1, 2, 3)]
        self.x_dev = (self.dx, self.f)
        self.y_dev = (self.dy, self.f)
        self.sib_dev = (self.d, self.sib)
        self.z_devs = [(self.d, 2 * zz + self.c) for zz in self.zs]

    def barrier(self):
        sem = pltpu.get_barrier_semaphore()
        for dev in [self.x_dev, self.y_dev, self.sib_dev] + self.z_devs:
            pl.semaphore_signal(sem, inc=1, device_id=dev, device_id_type=MESH)
        pl.semaphore_wait(sem, 6)


def remote(src, dst, send, recv, dev):
    return pltpu.make_async_remote_copy(src, dst, send, recv, device_id=dev, device_id_type=MESH)


class Gather:
    def __init__(self, at, shard, whole, send, recv):
        self.at, self.shard, self.whole, self.send, self.recv = at, shard, whole, send, recv
        self.chunks = whole.shape[0]

    def rows(self, zz, q, first, count):
        return pl.ds(pl.multiple_of((2 * zz + self.at.c) * 128 + 32 * q + first, 16), count)

    def push(self, k, rows, stage, dev, src=None):
        dst = self.whole.at[k, rows]
        remote(dst if src is None else src, dst, self.send.at[k], self.recv.at[k, stage], dev).start()

    def landed(self, k, stage, count):
        part = self.whole.at[k, pl.ds(0, count)]
        remote(part, part, self.send.at[k], self.recv.at[k, stage], self.at.x_dev).wait_recv()

    def begin(self, k):
        at = self.at
        quarter = self.shard.at[k, pl.ds(pl.multiple_of(32 * at.d, 16), 32)]
        for dev in at.z_devs:
            self.push(k, self.rows(at.z, at.d, 0, 32), 0, dev, quarter)
        self.push(k, self.rows(at.z, 0, 0, 128), 5, at.sib_dev, self.shard.at[k])

    def spread(self, k):
        at = self.at
        self.landed(k, 0, 96)
        for zz in at.zs:
            self.push(k, self.rows(zz, at.d, 0, 32), 1, at.x_dev)
            self.push(k, self.rows(zz, at.d, 0, 32), 2, at.y_dev)

    def diagonal(self, k):
        at = self.at
        self.landed(k, 1, 96)
        self.landed(k, 2, 96)
        for zz in at.zs:
            self.push(k, self.rows(zz, at.dx, 0, 16), 3, at.y_dev)
            self.push(k, self.rows(zz, at.dy, 16, 16), 4, at.x_dev)

    def pair(self, k):
        at = self.at
        self.landed(k, 3, 48)
        self.landed(k, 4, 48)
        for zz in at.zs:
            self.push(k, self.rows(zz, 0, 0, 128), 5, at.sib_dev)

    def ready(self, k):
        self.landed(k, 5, 512)

    def tick(self, t):
        if t + 3 < self.chunks:
            self.begin(t + 3)
        if 0 <= t - 2 < self.chunks:
            self.pair(t - 2)
        if 0 <= t - 1 < self.chunks:
            self.diagonal(t - 1)
        if 0 <= t < self.chunks:
            self.spread(t)

    def finish(self, k):
        part = self.whole.at[k, pl.ds(0, 896)]
        remote(part, part, self.send.at[k], self.recv.at[k, 0], self.at.x_dev).wait_send()


def spread_vectors(shards, vec, b_up):
    n = vec.shape[1] // 128
    for f in range(n):
        vec[:, 128 * f : 128 * (f + 1)] = shards[f, 0:8, :].astype(f32)
        for i in range(4):
            b_up[f : f + 1, 128 * i : 128 * (i + 1)] = shards[f, 8 + i : 9 + i, :].astype(f32)


def f1_kernel(rows, comm, *refs):
    if comm:
        (tok_h, ohy, ohx, tab, lab_col, lab_row, q_units, k_units, small, ws_h,
         x_h, normed_h, mixed_h, att_h, lse, mid_h, n2_h, vec, b_up, w_h,
         tok, acc, normed, w, mixed, att, bias, n2, lsem, wsem, osem, smalls, ssem, gsend, grecv) = refs
        at = Place()
        gather = Gather(at, ws_h, w_h, gsend, grecv)
        tick = gather.tick
    else:
        (tok_h, ohy, ohx, tab, lab_col, lab_row, q_units, k_units, vec_in, b_up_in, w_h,
         x_h, normed_h, mixed_h, att_h, lse, mid_h, n2_h, vec, b_up,
         tok, acc, normed, w, mixed, att, bias, n2, lsem, wsem, osem) = refs
        tick = lambda t: None
    pairs = rows // PAIR
    RB = PAIR // 7
    blocks = rows // RB

    def wcopy(k, s):
        return pltpu.make_async_copy(w_h.at[k], w.at[s], wsem.at[s])

    load = pltpu.make_async_copy(tok_h, tok, lsem.at[0])
    load.start()
    if comm:
        at.barrier()
        own = smalls.at[at.f]
        smalls[at.f] = small[...]
        for dev in at.z_devs:
            remote(own, own, ssem.at[0], ssem.at[1], dev).start()
        for k in range(3):
            gather.begin(k)
        keep = pltpu.make_async_copy(ws_h, w_h.at[:, pl.ds(pl.multiple_of(at.f * 128, 16), 128)], lsem.at[1])
        keep.start()
    else:
        wcopy(0, 0).start()
        vec[...] = vec_in[...]
        b_up[...] = b_up_in[...]
    fill_bias(bias, lab_col, lab_row, q_units, k_units)
    lse[...] = jnp.zeros_like(lse)
    load.wait()

    def place(r, carry):
        sl = pl.ds(pl.multiple_of(r * RB, 16), RB)
        py = dot(ohy[sl, :], tab[0]) + dot(ohy[sl, :], tab[1]) + dot(ohy[sl, :], tab[2])
        px = dot(ohx[sl, :], tab[0]) + dot(ohx[sl, :], tab[1]) + dot(ohx[sl, :], tab[2])
        acc[sl, :] = tok[sl, :].astype(f32) + jnp.concatenate([py, px], axis=1)
        return carry

    def norm_one(r, carry):
        sl = pl.ds(pl.multiple_of(r * RB, 16), RB)
        xhat, _ = norm_parts(acc[sl, :])
        normed[sl, :] = (xhat * vec[0:1, :] + vec[1:2, :]).astype(bf)
        return carry

    if comm:
        lax.fori_loop(0, blocks // 2, place, 0)
        three = smalls.at[pl.ds(0, 3)]
        remote(three, three, ssem.at[0], ssem.at[1], at.x_dev).wait()
        for zz in [at.z] + at.zs:
            slab = smalls.at[2 * zz + at.c]
            remote(slab, slab, ssem.at[2], ssem.at[3], at.sib_dev).start()
        tick(0)
        lax.fori_loop(blocks // 2, blocks, place, 0)
        four = smalls.at[pl.ds(0, 4)]
        remote(four, four, ssem.at[2], ssem.at[3], at.sib_dev).wait()
        spread_vectors(smalls, vec, b_up)
    else:
        lax.fori_loop(0, blocks, place, 0)
    x_out = pltpu.make_async_copy(acc, x_h, osem.at[0])
    x_out.start()
    tick(1)
    lax.fori_loop(0, blocks, norm_one, 0)
    tick(2)
    n_out = pltpu.make_async_copy(normed, normed_h, osem.at[1])
    n_out.start()
    if comm:
        keep.wait()

    for k in range(QUADS):
        s = k % 2
        if comm:
            gather.ready(k)
            wcopy(k, s).start()
        wcopy(k, s).wait()
        if not comm and k + 1 < QUADS:
            wcopy(k + 1, 1 - s).start()
        if k > 0:
            pltpu.make_async_copy(mixed, mixed_h.at[k - 1], osem.at[2]).wait()
            pltpu.make_async_copy(att, att_h.at[k - 1], osem.at[3]).wait()
        cols = slice(QW * k, QW * (k + 1))
        b_qkv = jnp.concatenate([vec[2:3, cols], jnp.zeros((1, QW), f32), vec[3:4, cols]], axis=1)

        def project(r, carry):
            sl = pl.ds(pl.multiple_of(r * PAIR, 16), PAIR)
            mixed[sl, :] = (dot(normed[sl, :], w[s, :, 0 : 3 * QW]) + b_qkv).astype(bf)
            return carry

        lax.fori_loop(0, pairs, project, 0)
        pltpu.make_async_copy(mixed, mixed_h.at[k], osem.at[2]).start()
        tick(3 + 3 * k)

        def hook(i):
            if comm:
                @pl.when(i == pairs - 1)
                def _():
                    tick(4 + 3 * k)

                @pl.when(i == 2 * pairs - 1)
                def _():
                    tick(5 + 3 * k)

        attention_forward(pairs, mixed, bias, att, lse, k, hook)
        pltpu.make_async_copy(att, att_h.at[k], osem.at[3]).start()
        if k == 0:
            x_out.wait()

        def project_out(r, carry):
            sl = pl.ds(pl.multiple_of(r * PAIR, 16), PAIR)
            extra = vec[4:5, :] if k == 0 else 0.0
            acc[sl, :] += dot(att[sl, :], w[s, :, 3 * QW : CW], NT) + extra
            return carry

        lax.fori_loop(0, pairs, project_out, 0)
    m_out = pltpu.make_async_copy(acc, mid_h, osem.at[0])
    m_out.start()

    def second(r, carry):
        sl = pl.ds(pl.multiple_of(r * RB, 16), RB)
        xhat, _ = norm_parts(acc[sl, :])
        n2[sl, :] = (xhat * vec[5:6, :] + vec[6:7, :]).astype(bf)
        return carry

    lax.fori_loop(0, blocks, second, 0)
    n2_out = pltpu.make_async_copy(n2, n2_h, osem.at[4])
    n2_out.start()
    pltpu.make_async_copy(mixed, mixed_h.at[QUADS - 1], osem.at[2]).wait()
    pltpu.make_async_copy(att, att_h.at[QUADS - 1], osem.at[3]).wait()
    n_out.wait()
    m_out.wait()
    n2_out.wait()
    if comm:
        for k in range(QUADS, gather.chunks):
            gather.ready(k)
        for k in range(gather.chunks):
            gather.finish(k)


def f1(rows, comm, chunks, *args):
    A, V = any_spec(), vmem_spec()
    out_shape = (sds((rows, D), f32), sds((rows, D), bf), sds((QUADS, rows, 3 * QW), bf), sds((QUADS, rows, QW), bf),
                 sds((rows, 128), f32), sds((rows, D), f32), sds((rows, D), bf), sds((8, D), f32), sds((8, FC), f32))
    out_specs = (A, A, A, A, V, A, A, V, V)
    scratch = [
        pltpu.VMEM((rows, D), bf), pltpu.VMEM((rows, D), f32), pltpu.VMEM((rows, D), bf), pltpu.VMEM((2, D, CW), bf),
        pltpu.VMEM((rows, 3 * QW), bf), pltpu.VMEM((rows, QW), bf), pltpu.VMEM((rows // PAIR * 4, QMAX, KEYS), f32),
        pltpu.VMEM((rows, D), bf),
        pltpu.SemaphoreType.DMA((2,)), pltpu.SemaphoreType.DMA((2,)), pltpu.SemaphoreType.DMA((5,)),
    ]
    in_specs = [A, V, V, V, V, V, V, V]
    if comm:
        in_specs += [V, A]
        out_shape += (sds((chunks, D, CW), bf),)
        out_specs += (A,)
        scratch += [pltpu.VMEM((8, 16, 128), bf), pltpu.SemaphoreType.DMA((4,)), pltpu.SemaphoreType.DMA((chunks,)),
                    pltpu.SemaphoreType.DMA((chunks, 6))]
        params = pltpu.CompilerParams(vmem_limit_bytes=VMEM_LIMIT, collective_id=0, has_side_effects=True)
    else:
        in_specs += [V, V, A]
        params = pltpu.CompilerParams(vmem_limit_bytes=VMEM_LIMIT)
    return pl.pallas_call(
        functools.partial(f1_kernel, rows, comm), out_shape=out_shape, in_specs=in_specs, out_specs=out_specs,
        scratch_shapes=scratch, compiler_params=params, name="attention_forward",
    )(*args)


def f2_kernel(rows, n2_h, g_h, mid_h, w_h, b_up, b_down, g2,
              out_h, gm_h, gb_h, gw_h, db_up, db_down, dg2, db2,
              n2, g, n2t, gt, w, act, dhid, acc_o, acc_d, gp, mid, ob, gb, lsem, wsem, osem, msem):
    KP = n2t.shape[1]
    NR = rows // PAIR
    first = QUADS
    chunks = w_h.shape[0] - QUADS

    def wcopy(j, s):
        return pltpu.make_async_copy(w_h.at[first + j], w.at[s], wsem.at[s])

    c1 = pltpu.make_async_copy(n2_h, n2, lsem.at[0])
    c1.start()
    c2 = pltpu.make_async_copy(g_h, g, lsem.at[1])
    c2.start()
    wcopy(0, 0).start()
    n2t[:, rows:KP] = jnp.zeros((D, KP - rows), bf)
    gt[:, rows:KP] = jnp.zeros((D, KP - rows), bf)
    act[rows:KP, :] = jnp.zeros((KP - rows, FC), bf)
    dhid[rows:KP, :] = jnp.zeros((KP - rows, FC), bf)
    acc_o[...] = jnp.zeros_like(acc_o)
    acc_d[...] = jnp.zeros_like(acc_d)
    c1.wait()
    c2.wait()
    transpose_rows(n2, n2t, rows)
    transpose_rows(g, gt, rows)

    def chunk(j, carry):
        s = lax.rem(j, 2)
        wcopy(j, s).wait()

        @pl.when(j + 1 < chunks)
        def _():
            wcopy(j + 1, 1 - s).start()

        def block(r, inner):
            sl = pl.ds(pl.multiple_of(r * PAIR, 16), PAIR)
            h = dot(n2[sl, :], w[s, :, 0:FC]) + b_up[pl.ds(j, 1), :]
            da = dot(g[sl, :], w[s, :, FC:CW])
            phi = 0.5 * (1.0 + lax.erf(h * 0.7071067811865476))
            slope = phi + h * (jnp.exp(-0.5 * h * h) * 0.3989422804014327)
            a = (h * phi).astype(bf)
            dh = (da * slope).astype(bf)
            act[sl, :] = a
            dhid[sl, :] = dh
            acc_o[sl, :] += dot(a, w[s, :, FC:CW], NT)
            acc_d[sl, :] += dot(dh, w[s, :, 0:FC], NT)
            return inner

        lax.fori_loop(0, NR, block, 0)
        db_up[pl.ds(j, 1), :] = dot(jnp.ones((8, KP), bf), dhid[...])[0:1]

        @pl.when(j > 0)
        def _():
            pltpu.make_async_copy(gp, gw_h.at[j - 1], osem.at[0]).wait()

        def grads(m, inner):
            sl = pl.ds(pl.multiple_of(m * 512, 512), 512)
            gp[sl, 0:FC] = dot(n2t[sl, :], dhid[...]).astype(bf)
            gp[sl, FC:CW] = dot(gt[sl, :], act[...]).astype(bf)
            return inner

        lax.fori_loop(0, D // 512, grads, 0)
        pltpu.make_async_copy(gp, gw_h.at[j], osem.at[0]).start()
        return carry

    lax.fori_loop(0, chunks, chunk, 0)
    RB = PAIR // 7
    blocks = rows // RB

    def mcopy(r, s):
        return pltpu.make_async_copy(mid_h.at[pl.ds(pl.multiple_of(r * RB, 16), RB)], mid.at[s], msem.at[s])

    mcopy(0, 0).start()
    dg2[...] = jnp.zeros_like(dg2)
    db2[...] = jnp.zeros_like(db2)
    db_down[...] = jnp.zeros_like(db_down)

    def last(r, carry):
        s = lax.rem(r, 2)
        sl = pl.ds(pl.multiple_of(r * RB, 16), RB)
        mcopy(r, s).wait()

        @pl.when(r + 1 < blocks)
        def _():
            mcopy(r + 1, 1 - s).start()

        middle = mid[s]
        ob[sl, :] = (middle + acc_o[sl, :] + b_down[...]).astype(bf)
        xhat, inv = norm_parts(middle)
        dn = acc_d[sl, :]
        cot = g[sl, :].astype(f32)
        e = dn * g2[...]
        gm = cot + (e - jnp.mean(e, axis=-1, keepdims=True) - xhat * jnp.mean(e * xhat, axis=-1, keepdims=True)) * inv
        acc_d[sl, :] = gm
        gb[sl, :] = gm.astype(bf)
        dg2[...] += jnp.sum(dn * xhat, axis=0, keepdims=True)
        db2[...] += jnp.sum(dn, axis=0, keepdims=True)
        db_down[...] += jnp.sum(cot, axis=0, keepdims=True)
        return carry

    lax.fori_loop(0, blocks, last, 0)
    outs = [pltpu.make_async_copy(acc_d, gm_h, osem.at[1]), pltpu.make_async_copy(ob, out_h, osem.at[2]),
            pltpu.make_async_copy(gb, gb_h, osem.at[3])]
    for o in outs:
        o.start()
    pltpu.make_async_copy(gp, gw_h.at[chunks - 1], osem.at[0]).wait()
    for o in outs:
        o.wait()


def f2(rows, n2, g, mid, w, b_up, b_down, g2):
    A, V = any_spec(), vmem_spec()
    KP = -(-rows // 256) * 256
    chunks = w.shape[0] - QUADS
    RB = PAIR // 7
    return pl.pallas_call(
        functools.partial(f2_kernel, rows),
        out_shape=(sds((rows, D), bf), sds((rows, D), f32), sds((rows, D), bf), sds((chunks, D, CW), bf), sds((chunks, FC), f32),
                   sds((1, D), f32), sds((1, D), f32), sds((1, D), f32)),
        in_specs=[A, A, A, A, V, V, V],
        out_specs=(A, A, A, A, V, V, V, V),
        scratch_shapes=[
            pltpu.VMEM((rows, D), bf), pltpu.VMEM((rows, D), bf), pltpu.VMEM((D, KP), bf), pltpu.VMEM((D, KP), bf),
            pltpu.VMEM((2, D, CW), bf), pltpu.VMEM((KP, FC), bf), pltpu.VMEM((KP, FC), bf),
            pltpu.VMEM((rows, D), f32), pltpu.VMEM((rows, D), f32), pltpu.VMEM((D, CW), bf),
            pltpu.VMEM((2, RB, D), f32), pltpu.VMEM((rows, D), bf), pltpu.VMEM((rows, D), bf),
            pltpu.SemaphoreType.DMA((2,)), pltpu.SemaphoreType.DMA((2,)), pltpu.SemaphoreType.DMA((4,)),
            pltpu.SemaphoreType.DMA((2,)),
        ],
        compiler_params=pltpu.CompilerParams(vmem_limit_bytes=VMEM_LIMIT),
        name="feed_forward",
    )(n2, g, mid, w, b_up, b_down, g2)


def attention_backward(pairs, mixed, datt, bias, lse, dmixed, dq, dk, dv, quad):
    def one(i, carry):
        p, hp = i // 2, lax.rem(i, 2)
        base = pl.multiple_of(p * PAIR, 16)
        lane0 = pl.multiple_of(hp * 128, 128)
        dq[...] = jnp.zeros_like(dq)
        dk[...] = jnp.zeros_like(dk)
        dv[...] = jnp.zeros_like(dv)
        for w, (start, halves) in enumerate(WINDOWS):
            for n, (q0, qn, k0) in enumerate(halves):
                at = start + q0
                row = pl.multiple_of(base + at, 16)
                kat = start + k0
                keys = pl.ds(pl.multiple_of(base + kat, 16), KEYS)
                q2 = mixed[pl.ds(row, qn), pl.ds(lane0, 128)] * jnp.asarray(SCALE, bf)
                k2 = mixed[keys, pl.ds(pl.multiple_of(lane0 + QW, 128), 128)]
                v2 = mixed[keys, pl.ds(pl.multiple_of(lane0 + 2 * QW, 128), 128)]
                do2 = datt[pl.ds(row, qn), pl.ds(lane0, 128)]
                lse_rows = lse[pl.ds(row, qn), :]
                lane = lax.broadcasted_iota(jnp.int32, (qn, 128), 1)
                idx = p * 4 + w * 2 + n
                dqs = None
                for h in range(2):
                    mask = half_mask(qn, h == 1)
                    kmask = half_mask(KEYS, h == 1)
                    qm = jnp.where(mask, q2, jnp.zeros_like(q2))
                    dom = jnp.where(mask, do2, jnp.zeros_like(do2))
                    head = quad * 4 + hp * 2 + h
                    row_lse = jnp.sum(jnp.where(lane == head, lse_rows, 0.0), axis=-1, keepdims=True)
                    s = dot(qm, k2, NT) + bias[idx, 0:qn, :]
                    probs = jnp.exp(s - row_lse)
                    dp = dot(dom, v2, NT)
                    inner = jnp.sum(probs * dp, axis=-1, keepdims=True)
                    ds = (probs * (dp - inner)).astype(bf)
                    dv[kat : kat + KEYS, :] += dot(probs.astype(bf), dom, TN)
                    dk[kat : kat + KEYS, :] += dot(ds, qm, TN)
                    part = dot(ds, k2)
                    dqs = part if h == 0 else jnp.where(mask, part, dqs)
                dq[at : at + qn, :] += dqs
        rows = pl.ds(base, PAIR)
        dmixed[rows, pl.ds(lane0, 128)] = (dq[...] * SCALE).astype(bf)
        dmixed[rows, pl.ds(pl.multiple_of(lane0 + QW, 128), 128)] = dk[...].astype(bf)
        dmixed[rows, pl.ds(pl.multiple_of(lane0 + 2 * QW, 128), 128)] = dv[...].astype(bf)
        return carry

    lax.fori_loop(0, pairs * 2, one, 0)


def f3_kernel(rows, gb_h, normed_h, w_h, mixed_h, att_h, lse, x_h, gm_h, g1, lab_col, lab_row, q_units, k_units,
              gt_h, gw_h, db_qkv, db_out, dg1, db1,
              gb, normed, gbt, normedt, w, mixed, att, datt, dmixed, bias, acc, dq, dk, dv, gp, xb, gmb, ob,
              lsem, wsem, isem, osem, xsem, gsem, tsem):
    KP = gbt.shape[1]
    pairs = rows // PAIR

    def inputs(k, s):
        return (pltpu.make_async_copy(w_h.at[k], w.at[s], wsem.at[s]),
                pltpu.make_async_copy(mixed_h.at[k], mixed.at[s], isem.at[s, 0]),
                pltpu.make_async_copy(att_h.at[k], att.at[s, pl.ds(0, rows)], isem.at[s, 1]))

    c1 = pltpu.make_async_copy(gb_h, gb, lsem.at[0])
    c1.start()
    c2 = pltpu.make_async_copy(normed_h, normed, lsem.at[1])
    c2.start()
    for c in inputs(0, 0):
        c.start()
    gbt[:, rows:KP] = jnp.zeros((D, KP - rows), bf)
    normedt[:, rows:KP] = jnp.zeros((D, KP - rows), bf)
    dmixed[rows:KP, :] = jnp.zeros((KP - rows, 3 * QW), bf)
    for s in range(2):
        att[s, rows:KP, :] = jnp.zeros((KP - rows, QW), bf)
    fill_bias(bias, lab_col, lab_row, q_units, k_units)
    c1.wait()
    c2.wait()
    transpose_rows(gb, gbt, rows)
    transpose_rows(normed, normedt, rows)
    db_out[...] = dot(jnp.ones((8, rows), bf), gb[...])[0:1]

    def quad(k, carry):
        s = lax.rem(k, 2)
        for c in inputs(k, s):
            c.wait()

        @pl.when(k + 1 < QUADS)
        def _():
            for c in inputs(k + 1, 1 - s):
                c.start()

        def back(r, inner):
            sl = pl.ds(pl.multiple_of(r * PAIR, 16), PAIR)
            datt[sl, :] = dot(gb[sl, :], w[s, :, 3 * QW : CW]).astype(bf)
            return inner

        lax.fori_loop(0, pairs, back, 0)
        attention_backward(pairs, mixed.at[s], datt, bias, lse, dmixed, dq, dk, dv, k)
        db_qkv[pl.ds(k, 1), :] = dot(jnp.ones((8, KP), bf), dmixed[...])[0:1]

        @pl.when(k > 0)
        def _():
            pltpu.make_async_copy(gp, gw_h.at[k - 1], osem.at[0]).wait()

        def grads(m, inner):
            sl = pl.ds(pl.multiple_of(m * 512, 512), 512)
            gp[sl, 0 : 3 * QW] = dot(normedt[sl, :], dmixed[...]).astype(bf)
            gp[sl, 3 * QW : CW] = dot(gbt[sl, :], att[s]).astype(bf)
            return inner

        lax.fori_loop(0, D // 512, grads, 0)
        pltpu.make_async_copy(gp, gw_h.at[k], osem.at[0]).start()

        def back_in(r, inner):
            sl = pl.ds(pl.multiple_of(r * PAIR, 16), PAIR)
            new = dot(dmixed[sl, :], w[s, :, 0 : 3 * QW], NT)
            acc[sl, :] = jnp.where(k == 0, new, acc[sl, :] + new)
            return inner

        lax.fori_loop(0, pairs, back_in, 0)
        return carry

    lax.fori_loop(0, QUADS, quad, 0)
    RB = PAIR // 7
    blocks = rows // RB

    def part(r):
        return pl.ds(pl.multiple_of(r * RB, 16), RB)

    def rcopies(r, s):
        return (pltpu.make_async_copy(x_h.at[part(r)], xb.at[s], xsem.at[s]),
                pltpu.make_async_copy(gm_h.at[part(r)], gmb.at[s], gsem.at[s]))

    for c in rcopies(0, 0):
        c.start()
    dg1[...] = jnp.zeros_like(dg1)
    db1[...] = jnp.zeros_like(db1)

    def last(r, carry):
        s = lax.rem(r, 2)
        for c in rcopies(r, s):
            c.wait()

        @pl.when(r + 1 < blocks)
        def _():
            for c in rcopies(r + 1, 1 - s):
                c.start()

        @pl.when(r >= 2)
        def _():
            pltpu.make_async_copy(ob.at[s], gt_h.at[part(r - 2)], tsem.at[s]).wait()

        xhat, inv = norm_parts(xb[s])
        dn = acc[part(r), :]
        e = dn * g1[...]
        ob[s] = gmb[s] + (e - jnp.mean(e, axis=-1, keepdims=True) - xhat * jnp.mean(e * xhat, axis=-1, keepdims=True)) * inv
        pltpu.make_async_copy(ob.at[s], gt_h.at[part(r)], tsem.at[s]).start()
        dg1[...] += jnp.sum(dn * xhat, axis=0, keepdims=True)
        db1[...] += jnp.sum(dn, axis=0, keepdims=True)
        return carry

    lax.fori_loop(0, blocks, last, 0)
    for r in (blocks - 2, blocks - 1):
        pltpu.make_async_copy(ob.at[r % 2], gt_h.at[part(r)], tsem.at[r % 2]).wait()
    pltpu.make_async_copy(gp, gw_h.at[QUADS - 1], osem.at[0]).wait()


def f3(rows, gb, normed, w, mixed, att, lse, x, gm, g1, lab_col, lab_row, q_units, k_units):
    A, V = any_spec(), vmem_spec()
    KP = -(-rows // 256) * 256
    RB = PAIR // 7
    return pl.pallas_call(
        functools.partial(f3_kernel, rows),
        out_shape=(sds((rows, D), f32), sds((QUADS, D, CW), bf), sds((QUADS, 3 * QW), f32), sds((1, D), f32), sds((1, D), f32),
                   sds((1, D), f32)),
        in_specs=[A, A, A, A, A, V, A, A, V, V, V, V, V],
        out_specs=(A, A, V, V, V, V),
        scratch_shapes=[
            pltpu.VMEM((rows, D), bf), pltpu.VMEM((rows, D), bf), pltpu.VMEM((D, KP), bf), pltpu.VMEM((D, KP), bf),
            pltpu.VMEM((2, D, CW), bf), pltpu.VMEM((2, rows, 3 * QW), bf), pltpu.VMEM((2, KP, QW), bf), pltpu.VMEM((rows, QW), bf),
            pltpu.VMEM((KP, 3 * QW), bf), pltpu.VMEM((rows // PAIR * 4, QMAX, KEYS), f32), pltpu.VMEM((rows, D), f32),
            pltpu.VMEM((PAIR, 128), f32), pltpu.VMEM((PAIR, 128), f32), pltpu.VMEM((PAIR, 128), f32), pltpu.VMEM((D, CW), bf),
            pltpu.VMEM((2, RB, D), f32), pltpu.VMEM((2, RB, D), f32), pltpu.VMEM((2, RB, D), f32),
            pltpu.SemaphoreType.DMA((2,)), pltpu.SemaphoreType.DMA((2,)), pltpu.SemaphoreType.DMA((2, 2)),
            pltpu.SemaphoreType.DMA((1,)), pltpu.SemaphoreType.DMA((2,)), pltpu.SemaphoreType.DMA((2,)),
            pltpu.SemaphoreType.DMA((2,)),
        ],
        compiler_params=pltpu.CompilerParams(vmem_limit_bytes=VMEM_LIMIT),
        name="attention_backward",
    )(gb, normed, w, mixed, att, lse, x, gm, g1, lab_col, lab_row, q_units, k_units)


def unit_labels(band_code):
    units = band_code.reshape(-1, UNITS_MB)
    labels = jnp.cumsum((units <= 1).astype(jnp.int32), axis=1) + 16 * jnp.arange(units.shape[0], dtype=jnp.int32)[:, None]
    return labels.reshape(-1).astype(f32)


def window_units(rows):
    units = rows // UNIT
    queries, keys = [], []
    for p in range(rows // PAIR):
        for w, (start, halves) in enumerate(WINDOWS):
            for q0, qn, k0 in halves:
                q = p * PAIR + start + q0 + np.arange(QMAX)
                inside = (q >= p * PAIR + w * BUF) & (q < p * PAIR + (w + 1) * BUF)
                queries.append((q[:, None] // UNIT == np.arange(units)) & inside[:, None])
                k = p * PAIR + start + k0 + np.arange(KEYS)
                keys.append(np.arange(units)[:, None] == k // UNIT)
    return jnp.asarray(np.stack(queries), bf), jnp.asarray(np.stack(keys), bf)


def place_table(gsd_code):
    ratio = jnp.exp2((gsd_code.astype(f32) - 3.0) * 0.5)
    quarter = D // 4
    freq = jnp.exp2(jnp.arange(quarter, dtype=f32) * (-math.log2(10000.0) / quarter))
    a = jnp.arange(GRID, dtype=f32)
    angle = (a[None, :] * ratio[:, None]).reshape(-1)[:, None] * freq[None, :]
    tab = jnp.concatenate([jnp.sin(angle), jnp.cos(angle)], axis=1)
    n = tab.shape[0]
    pad = -(-n // 256) * 256
    tab = jnp.pad(tab, ((0, pad - n), (0, 0)))
    hi = lax.reduce_precision(tab, 8, 7)
    rest = tab - hi
    mid = lax.reduce_precision(rest, 8, 7)
    return jnp.stack([hi, mid, rest - mid]).astype(bf)


def one_hots(rows, width):
    r = np.arange(rows)
    col = np.arange(width)
    ohy = (r[:, None] // GRID == col[None, :])
    ohx = ((r // UNIT * GRID + r % GRID)[:, None] == col[None, :])
    return jnp.asarray(ohy, bf), jnp.asarray(ohx, bf)


def pack_weights(qkv, out, up, down):
    n = qkv.shape[0]
    att = jnp.concatenate([qkv.reshape(n, 3, QUADS, QW).transpose(2, 0, 1, 3).reshape(QUADS, n, 3 * QW),
                           out.T.reshape(n, QUADS, QW).transpose(1, 0, 2)], axis=2)
    ff = up.shape[1] // FC
    feed = jnp.concatenate([up.reshape(n, ff, FC).transpose(1, 0, 2), down.T.reshape(n, ff, FC).transpose(1, 0, 2)], axis=2)
    return jnp.concatenate([att, feed], axis=0)


def local(dp, fsdp, tokens, band_code, gsd_code, norm1_gain, norm1_bias, qkv_weight, bias_q, bias_v, out_weight, bias_out,
          norm2_gain, norm2_bias, up_weight, bias_up, down_weight, bias_down, grad_out):
    rows = tokens.shape[0]
    comm = dp == 4 and fsdp == 8
    shard = pack_weights(qkv_weight, out_weight, up_weight, down_weight)
    n = shard.shape[1]
    chunks = shard.shape[0]
    vectors = (norm1_gain, norm1_bias, bias_q, bias_v, bias_out, norm2_gain, norm2_bias, bias_down)
    labels = unit_labels(band_code)
    tab = place_table(gsd_code)
    ohy, ohx = one_hots(rows, tab.shape[1])
    q_units, k_units = window_units(rows)
    lab = (labels.reshape(-1, 1), labels.reshape(1, -1), q_units, k_units)
    if comm:
        small = jnp.concatenate([jnp.stack(vectors), bias_up.reshape(4, 128), jnp.zeros((4, 128), bf)])
        x, normed, mixed, att, lse, mid, n2, vec, b_up, w = f1(rows, True, chunks, tokens, ohy, ohx, tab, *lab, small, shard)
    else:
        gathered = lax.all_gather(jnp.stack(vectors), "fsdp", axis=1, tiled=True).astype(f32)
        up_bias = lax.all_gather(bias_up, "fsdp", axis=0, tiled=True).astype(f32).reshape(-1, FC)
        w = lax.all_gather(shard, "fsdp", axis=1, tiled=True)
        x, normed, mixed, att, lse, mid, n2, vec, b_up = f1(rows, False, chunks, tokens, ohy, ohx, tab, *lab, gathered, up_bias, w)
    out, gm, gb, gw_ff, db_up, db_down, dg2, db2 = f2(rows, n2, grad_out, mid, w, b_up, vec[7:8], vec[5:6])
    grad_tokens, gw_att, db_qkv, db_out, dg1, db1 = f3(rows, gb, normed, w, mixed, att, lse, x, gm, vec[0:1], *lab)
    small_grads = jnp.concatenate([dg1, db1, db_qkv[:, 0:QW].reshape(1, D), db_qkv[:, 2 * QW :].reshape(1, D), db_out, dg2, db2,
                                   db_down], axis=0)
    small_grads = jnp.concatenate([small_grads.reshape(8, fsdp, n).transpose(1, 0, 2).reshape(fsdp, 8 * n),
                                   db_up.reshape(fsdp, 4 * n)], axis=1)
    gw = jnp.concatenate([gw_att, gw_ff], axis=0)
    gw = lax.psum(lax.psum_scatter(gw, "fsdp", scatter_dimension=1, tiled=True), "dp").astype(f32)
    sg = lax.psum(lax.psum_scatter(small_grads, "fsdp", scatter_dimension=0, tiled=True), "dp").reshape(12, n)
    g_att, g_ff = gw[:QUADS], gw[QUADS:]
    g_qkv = g_att[:, :, : 3 * QW].reshape(QUADS, n, 3, QW).transpose(1, 2, 0, 3).reshape(n, 3 * D)
    g_out = g_att[:, :, 3 * QW :].transpose(0, 2, 1).reshape(D, n)
    g_up = g_ff[:, :, :FC].transpose(1, 0, 2).reshape(n, -1)
    g_down = g_ff[:, :, FC:].transpose(0, 2, 1).reshape(-1, n)
    return (out, grad_tokens, sg[0], sg[1], g_qkv, sg[2], sg[3], g_out, sg[4], sg[5], sg[6], g_up, sg[8:12].reshape(4 * n), g_down, sg[7])


def solution(mesh):
    rows, vec, first, second = P(("dp", "fsdp"), None), P("fsdp"), P("fsdp", None), P(None, "fsdp")
    codes = P(("dp", "fsdp"))
    return jax.shard_map(
        functools.partial(local, mesh.shape["dp"], mesh.shape["fsdp"]),
        mesh=mesh,
        in_specs=(rows, codes, codes, vec, vec, first, vec, vec, second, vec, vec, vec, first, vec, second, vec, rows),
        out_specs=(rows, rows, vec, vec, first, vec, vec, second, vec, vec, vec, first, vec, second, vec),
        check_vma=False,
    )
```

time: 1660 us -> 859 us (0.52)
  matrix products: 488 us -> 0 us
  Pallas kernels: 0 us -> 443 us
  waiting for transfers between devices: 708 us -> 295 us
  other arithmetic: 188 us -> 29.1 us
  blocking collectives: 130 us -> 36.6 us
  local copies, waits for them, and re-layouts: 95.7 us -> 29.4 us
  loops' own time: 25.1 us -> 0 us
    dot_general x76 -> x0, matrix products: 488 us -> none  [the longest x8 62 us: attention_scores(): jnp.einsum('qhe,khe->hqk', queries, keys_all, preferred_element_type=jnp....]
    pallas_call x0 -> x3, Pallas kernels: none -> 443 us  [the longest x1 192 us: f1(): pl.pallas_call(functools.partial(f1_kernel, rows, comm), out_shape=out_sh...]
    reduce_scatter x4 -> x1, waiting for transfers between devices: 507 us -> 245 us  [local(): lax.psum_scatter(gw, 'fsdp', scatter_dimension=1, tiled=True)]
    all_gather x4 -> x0, waiting for transfers between devices: 153 us -> none  [the longest x1 82.5 us: local(): lax.all_gather(down_weight, 'fsdp', axis=1, tiled=True)]
    all_gather x9 -> x0, blocking collectives: 92.9 us -> none  [the longest x1 13.5 us: local(): lax.all_gather(norm1_gain, 'fsdp', axis=0, tiled=True)]
    convert_element_type x77 -> x3, other arithmetic: 60.7 us -> 3.37 us  [the longest x1 2.64 us: local(): lax.psum(lax.psum_scatter(gw, 'fsdp', scatter_dimension=1, tiled=True), '...]
    reduce_sum x44 -> x0, other arithmetic: 55.1 us -> none  [the longest x20 24.7 us: layer_norm(): center = row_block - jnp.mean(row_block, axis=-1, keepdims=True)]
    dynamic_update_slice x20 -> x0, other arithmetic: 51.8 us -> none  [local(): lax.map(lambda pieces: forward_block(gathered, pieces[0], pieces[1], piec...]
  transfers between devices with their start and end apart: 9 -> 2, of which waited for: 7 -> 2; matrix products, arithmetic and copies ran while one was open for 2% -> 0% of each run, Pallas kernels for 0% -> 0%
where the time goes in v1:
time: 859 us; the launch traced here: 848 us
  Pallas kernels  443 us (52%)
  waiting for transfers between devices  295 us (34%)
  blocking collectives  36.6 us (4%)
  local copies, waits for them, and re-layouts  29.4 us (3%)
  other arithmetic  29.1 us (3%)
  between operations  15 us (2%)
    reduce_scatter x1, waiting for transfers between devices, local(): lax.psum_scatter(gw, 'fsdp', scatter_dimension=1, tiled=True)  245 us
    pallas_call x1, Pallas kernels, f1(): pl.pallas_call(functools.partial(f1_kernel, rows, comm), out_shape=out_sh...  192 us
    pallas_call x1, Pallas kernels, f3(): pl.pallas_call(functools.partial(f3_kernel, rows), out_shape=(sds((rows,...  131 us
    pallas_call x1, Pallas kernels, f2(): pl.pallas_call(functools.partial(f2_kernel, rows), out_shape=(sds((rows,...  120 us
    psum x1, waiting for transfers between devices, local(): lax.psum(lax.psum_scatter(gw, 'fsdp', scatter_dimension=1, tiled=True), '...  49.5 us
    unnamed x1, blocking collectives  26.3 us
    concatenate x1, other arithmetic, local(): gw = jnp.concatenate([gw_att, gw_ff], axis=0)  21 us
  transfers between devices with their start and end apart: 2, of which 2 were waited for; matrix products, arithmetic and copies ran while one was open for 0% of the time, Pallas kernels for 0%

profile of v1, /device:TPU:0, one launch (start us, length us, event | category | flops | bytes accessed | tf_op | source)
XLA Modules:
  0.0 847.9 jit_solution(156590792792845163)
XLA Ops:
  10.4 1.5 copy.68
  12.3 1.7 copy.72
  14.5 1.5 copy.74
  17.1 1.0 pad_maximum_fusion.1.refs_3_
  18.1 1.9 maximum_maximum_fusion.refs_9_
  20.1 1.2 concatenate.42.refs_8_
  21.3 192.2 %attention_forward.1 = (f32[1568,1024]{1,0:T(8,128)}, bf16[1568,1024]{1,0:T(8,128)(2,1)}, bf16[4,1568,768]{2,1,0:T(8,128)(2,1)}, bf16[4,1568,256]{2,1,0:T(8,128)...) custom-call(bf16[1568,1024]{1,0:T(8,128)(2,1)} %refs_0_.1, ...), custom_call_target="tpu_custom_call" | custom-call | tf_op jit(solution)/shard_map/attention_forward/pallas_call | solution.py:402
  213.6 1.5 fusion.4
  215.0 120.2 %feed_forward.1 = (bf16[1568,1024]{1,0:T(8,128)(2,1)}, f32[1568,1024]{1,0:T(8,128)}, bf16[1568,1024]{1,0:T(8,128)(2,1)}, bf16[8,1024,1024]{2,1,0:T(8,128)(2,1)},...) custom-call(bf16[1568,1024]{1,0:T(8,128)(2,1)} %get-tuple-element.39.n2_h, ...), custom_call_target="tpu_custom_call" | custom-call | tf_op jit(solution)/shard_map/feed_forward/pallas_call | solution.py:524
  335.2 130.7 %attention_backward.1 = (f32[1568,1024]{1,0:T(8,128)}, bf16[4,1024,1024]{2,1,0:T(8,128)(2,1)}, f32[4,768]{1,0:T(4,128)}, f32[1,1024]{1,0:T(1,128)}, f32[1,1024]{1,0:T(1,128)}, /*index=5*/f32[1,1024]{1,0:T(1,128)}) custom-call(bf16[1568,1024]{1,0:T(8,128)(2,1)} %get-tuple-element.45.gb_h, bf16[1568,1024]{1,0:T(8,128)(2,1)} %get-tuple-element.46.normed_h, ...), custom_call_target="tpu_custom_call" | custom-call | tf_op jit(solution)/shard_map/attention_backward/pallas_call | solution.py:711
  465.9 21.0 %pad_maximum_fusion = bf16[12,1024,1024]{2,1,0:T(8,128)(2,1)} fusion(bf16[8,1024,1024]{2,1,0:T(8,128)(2,1)} %get-tuple-element.62, bf16[4,1024,1024]{2,1,0:T(8,128)(2,1)} %get-tuple-element.61), kind=kLoop, calls=%fused_computation | loop fusion | flops 12582912 | bytes 50331648 | tf_op jit(solution)/shard_map/concatenate | solution.py:812
  487.0 245.1 %reduce-scatter.2.cloned.1.call-done = bf16[12,128,1024]{2,1,0:T(8,128)(2,1)} async-done(((bf16[12,1024,1024]{2,1,0:T(8,128)(2,1)}), bf16[12,128,1024]{2,1,0:T(8,128)(2,1)}) %reduce-scatter.2.cloned.1.call-update) | async-done | bytes 3145744 | tf_op jit(solution)/shard_map/reduce_scatter | solution.py:813
  733.0 26.3 %all-reduce.1 = f32[8,1536]{1,0:T(8,128)S(1)} all-reduce(f32[8,1536]{1,0:T(8,128)S(1)} %pad_maximum_fusion.2), channel_id=2, replica_groups=mesh['dp'=4,'fsdp'=8] {'fsdp'}, use_global_device_ids=true, to_apply=%region_1.2.clone | all-reduce | flops 12288 | bytes 98304
  760.0 10.2 %psum.14 = f32[1,1536]{1,0:T(1,128)S(1)} all-reduce(f32[1,1536]{1,0:T(1,128)S(1)} %constant_dynamic-slice_fusion), channel_id=1, replica_groups=mesh['dp'=4,'fsdp'=8] {'dp'}, use_global_device_ids=true, to_apply=%region_2.3 | all-reduce | flops 1536 | bytes 12288 | tf_op jit(solution)/shard_map/psum | solution.py:814
  771.3 49.5 %all-reduce.4.cloned.1.call-done = bf16[12,128,1024]{2,1,0:T(8,128)(2,1)} async-done(((bf16[12,128,1024]{2,1,0:T(8,128)(2,1)}), bf16[12,128,1024]{2,1,0:T(8,128)(2,1)}) %all-reduce.4.cloned.1.call-update) | async-done | bytes 3145744 | tf_op jit(solution)/shard_map/psum | solution.py:813
  820.8 2.6 convert_element_type.44
  823.5 2.6 slice_bitcast_fusion
  826.9 1.9 copy.80
  828.8 1.8 copy.83
  830.7 3.0 copy.81
  833.7 2.0 copy.79
  835.7 1.3 slice.89
  837.0 1.9 copy.77
  839.0 1.6 copy.82
  (80 shorter events, 8.7 us)
Async XLA Ops:
  7.2 725.0 %reduce-scatter.2.cloned.1.call-start = ((), (), s32[]{:S(2)}) async-start(), calls=%async_computation.1 | async-start | bytes 28311552 | tf_op jit(solution)/shard_map/reduce_scatter | solution.py:813
  12.2 3.7 copy-start.1
  18.1 2.0 copy-start.10
  18.1 2.0 copy-start.11
  18.1 2.0 copy-start.12
  18.1 2.0 copy-start.13
  18.1 2.0 copy-start.14
  18.1 2.0 copy-start.15
  18.1 2.0 copy-start.16
  18.1 2.0 copy-start.17
  18.1 2.0 copy-start.18
  486.9 245.3 %copy-start.3 = (f32[4,768]{1,0:T(4,128)S(1)}, f32[4,768]{1,0:T(4,128)}, u32[]{:S(2)}) copy-start(f32[4,768]{1,0:T(4,128)} %get-tuple-element.55) | copy-start | bytes 36868
  486.9 245.3 %copy-start.19 = (u32[32]{0:T(128)S(1)}, u32[32]{0:T(128)}, u32[]{:S(2)}) copy-start(u32[32]{0:T(128)} %constant.40) | copy-start | bytes 388
  486.9 245.9 %copy-start.9 = (f32[1,1024]{1,0:T(1,128)S(1)}, f32[1,1024]{1,0:T(1,128)}, u32[]{:S(2)}) copy-start(f32[1,1024]{1,0:T(1,128)} %get-tuple-element.53) | copy-start | bytes 12292
  486.9 245.9 %copy-start.8 = (f32[1,1024]{1,0:T(1,128)S(1)}, f32[1,1024]{1,0:T(1,128)}, u32[]{:S(2)}) copy-start(f32[1,1024]{1,0:T(1,128)} %get-tuple-element.54) | copy-start | bytes 12292
  486.9 245.9 %copy-start.7 = (f32[1,1024]{1,0:T(1,128)S(1)}, f32[1,1024]{1,0:T(1,128)}, u32[]{:S(2)}) copy-start(f32[1,1024]{1,0:T(1,128)} %get-tuple-element.56) | copy-start | bytes 12292
  486.9 245.9 %copy-start.6 = (f32[1,1024]{1,0:T(1,128)S(1)}, f32[1,1024]{1,0:T(1,128)}, u32[]{:S(2)}) copy-start(f32[1,1024]{1,0:T(1,128)} %get-tuple-element.57) | copy-start | bytes 12292
  486.9 245.9 %copy-start.5 = (f32[1,1024]{1,0:T(1,128)S(1)}, f32[1,1024]{1,0:T(1,128)}, u32[]{:S(2)}) copy-start(f32[1,1024]{1,0:T(1,128)} %get-tuple-element.58) | copy-start | bytes 12292
  487.0 246.0 %copy-start.4 = (f32[1,1024]{1,0:T(1,128)S(1)}, f32[1,1024]{1,0:T(1,128)}, u32[]{:S(2)}) copy-start(f32[1,1024]{1,0:T(1,128)} %get-tuple-element.59) | copy-start | bytes 12292
  487.0 246.0 %copy-start.2 = (f32[8,512]{1,0:T(8,128)S(1)}, f32[8,512]{1,0:T(8,128)}, u32[]{:S(2)}) copy-start(f32[8,512]{1,0:T(8,128)} %get-tuple-element.60) | copy-start | bytes 49156
  487.0 333.8 %all-reduce.4.cloned.1.call-start = ((), (), s32[]{:S(2)}) async-start(), calls=%async_computation.2 | async-start | bytes 6291456 | tf_op jit(solution)/shard_map/psum | solution.py:813
  830.7 5.1 copy-start
Sparse Core Ops, SparseCore 0:
  487.0 245.0 reduce-scatter.1
  735.2 85.5 all-reduce.3

commit v2 on v1

--- a/solution.py
+++ b/solution.py
@@ -133,6 +133,16 @@
 MESH = pl.DeviceIdType.MESH
 
 
+def kernel_params(comm, number):
+    if comm:
+        return pltpu.CompilerParams(vmem_limit_bytes=VMEM_LIMIT, collective_id=number, has_side_effects=True)
+    return pltpu.CompilerParams(vmem_limit_bytes=VMEM_LIMIT)
+
+
+def grad_shape(comm, chunks):
+    return sds((chunks, 128, CW) if comm else (chunks, 4, 256, CW), bf)
+
+
 class Place:
     def __init__(self):
         self.d = lax.axis_index("dp")
@@ -395,19 +405,175 @@
         out_specs += (A,)
         scratch += [pltpu.VMEM((8, 16, 128), bf), pltpu.SemaphoreType.DMA((4,)), pltpu.SemaphoreType.DMA((chunks,)),
                     pltpu.SemaphoreType.DMA((chunks, 6))]
-        params = pltpu.CompilerParams(vmem_limit_bytes=VMEM_LIMIT, collective_id=0, has_side_effects=True)
     else:
         in_specs += [V, V, A]
-        params = pltpu.CompilerParams(vmem_limit_bytes=VMEM_LIMIT)
     return pl.pallas_call(
         functools.partial(f1_kernel, rows, comm), out_shape=out_shape, in_specs=in_specs, out_specs=out_specs,
-        scratch_shapes=scratch, compiler_params=params, name="attention_forward",
+        scratch_shapes=scratch, compiler_params=kernel_params(comm, 0), name="attention_forward",
     )(*args)
 
 
-def f2_kernel(rows, n2_h, g_h, mid_h, w_h, b_up, b_down, g2,
+class Reduce:
+    SLOTS = 3
+    STEPS = ((12, "done"), (10, "share"), (9, "total"), (7, "planes"), (4, "relay"), (1, "cross"), (0, "pair"))
+
+    def __init__(self, at, count, gp, r1, rx, ry, rz, fin, out, send, recv, osem, sizes):
+        self.at, self.count, self.gp, self.r1, self.rx, self.ry, self.rz = at, count, gp, r1, rx, ry, rz
+        self.fin, self.out, self.send, self.recv, self.osem, self.sizes = fin, out, send, recv, osem, sizes
+
+    @classmethod
+    def scratch(cls, count):
+        s = cls.SLOTS
+        return [pltpu.VMEM((s, 4, 256, CW), bf), pltpu.VMEM((s, 4, 128, CW), bf), pltpu.VMEM((s, 3, 4, 16, CW), bf),
+                pltpu.VMEM((s, 3, 4, 16, CW), bf), pltpu.VMEM((s, 3, 32, CW), bf), pltpu.VMEM((count, 32, CW), bf),
+                pltpu.SemaphoreType.DMA((count, 2)), pltpu.SemaphoreType.DMA((count, 6)), pltpu.SemaphoreType.DMA((count,))]
+
+    def slot(self, t):
+        return lax.rem(t, self.SLOTS)
+
+    def rows(self, q, first, count):
+        return pl.ds(pl.multiple_of(self.at.c * 128 + q * 32 + first, 16), count)
+
+    def push(self, t, src, dst, stage, dev, group=0):
+        remote(src, dst, self.send.at[t, group], self.recv.at[t, stage], dev).start()
+
+    def landed(self, t, stage, rows):
+        part = self.sizes.at[0, pl.ds(0, rows)]
+        remote(part, part, self.send.at[t, 0], self.recv.at[t, stage], self.at.x_dev).wait_recv()
+
+    def left(self, t, group, rows):
+        part = self.sizes.at[0, pl.ds(0, rows)]
+        remote(part, part, self.send.at[t, group], self.recv.at[t, 0], self.at.x_dev).wait_send()
+
+    def add(self, t, q, first, *parts):
+        s, sl = self.slot(t), self.rows(q, first, 16)
+        total = self.gp[s, :, sl, :].astype(f32)
+        for p in parts:
+            total = total + p.astype(f32)
+        self.gp[s, :, sl, :] = total.astype(bf)
+
+    def pair(self, t):
+        s = self.slot(t)
+        other = pl.ds(pl.multiple_of((1 - self.at.c) * 128, 128), 128)
+        self.push(t, self.gp.at[s, :, other], self.r1.at[s], 0, self.at.sib_dev)
+
+    def cross(self, t):
+        at, s = self.at, self.slot(t)
+        self.landed(t, 0, 512)
+        own = pl.ds(pl.multiple_of(at.c * 128, 128), 128)
+
+        def plane(zz, carry):
+            self.gp[s, zz, own, :] = (self.gp[s, zz, own, :].astype(f32) + self.r1[s, zz].astype(f32)).astype(bf)
+            return carry
+
+        lax.fori_loop(0, 4, plane, 0)
+        gp = self.gp
+        self.push(t, gp.at[s, :, self.rows(at.dd, 0, 16)], self.rx.at[s, 0], 1, at.x_dev)
+        self.push(t, gp.at[s, :, self.rows(at.dd, 16, 16)], self.ry.at[s, 0], 1, at.y_dev)
+        self.push(t, gp.at[s, :, self.rows(at.dx, 0, 16)], self.rx.at[s, 1], 2, at.x_dev)
+        self.push(t, gp.at[s, :, self.rows(at.dy, 16, 16)], self.ry.at[s, 1], 2, at.y_dev)
+
+    def relay(self, t):
+        at, s = self.at, self.slot(t)
+        self.landed(t, 1, 128)
+        self.add(t, at.dy, 0, self.rx[s, 0])
+        self.add(t, at.dx, 16, self.ry[s, 0])
+        self.push(t, self.gp.at[s, :, self.rows(at.dy, 0, 16)], self.ry.at[s, 2], 2, at.y_dev)
+        self.push(t, self.gp.at[s, :, self.rows(at.dx, 16, 16)], self.rx.at[s, 2], 2, at.x_dev)
+
+    def planes(self, t):
+        at, s = self.at, self.slot(t)
+        self.landed(t, 2, 256)
+        self.add(t, at.d, 0, self.rx[s, 1], self.ry[s, 2])
+        self.add(t, at.d, 16, self.ry[s, 1], self.rx[s, 2])
+        for n, (zz, dev) in enumerate(zip(at.zs, at.z_devs)):
+            self.push(t, self.gp.at[s, zz, self.rows(at.d, 0, 32)], self.rz.at[s, n], 3, dev)
+
+    def quarter(self, t, q, first=0, count=32):
+        return self.out.at[t, pl.ds(pl.multiple_of(q * 32 + first, 16), count)]
+
+    def total(self, t):
+        at, s = self.at, self.slot(t)
+        self.landed(t, 3, 96)
+        total = self.gp[s, at.z, self.rows(at.d, 0, 32), :].astype(f32)
+        for n in range(3):
+            total = total + self.rz[s, n].astype(f32)
+        self.fin[t] = total.astype(bf)
+        pltpu.make_async_copy(self.fin.at[t], self.quarter(t, at.d), self.osem.at[t]).start()
+        self.push(t, self.fin.at[t], self.quarter(t, at.d), 4, at.x_dev, 1)
+        self.push(t, self.fin.at[t], self.quarter(t, at.d), 4, at.y_dev, 1)
+
+    def share(self, t):
+        at = self.at
+        self.landed(t, 4, 64)
+        self.push(t, self.quarter(t, at.dx, 0, 16), self.quarter(t, at.dx, 0, 16), 5, at.y_dev, 1)
+        self.push(t, self.quarter(t, at.dy, 16, 16), self.quarter(t, at.dy, 16, 16), 5, at.x_dev, 1)
+
+    def done(self, t):
+        self.landed(t, 5, 32)
+        self.left(t, 1, 96)
+        pltpu.make_async_copy(self.fin.at[t], self.quarter(t, self.at.d), self.osem.at[t]).wait()
+
+    def release(self, t):
+        self.left(t, 0, 992)
+
+    def tick(self, j, i):
+        for offset, name in self.STEPS:
+            if offset % 4 == i:
+                t = j - offset // 4
+                if isinstance(t, int):
+                    if 0 <= t < self.count:
+                        getattr(self, name)(t)
+                else:
+                    pl.when((t >= 0) & (t < self.count))(functools.partial(getattr(self, name), t))
+
+    def drain(self, j, i, last):
+        for k in range(4 * j + i, 4 * (last + 3) + 1):
+            self.tick(k // 4, k % 4)
+
+
+class Keep:
+    SLOTS = 3
+
+    def __init__(self, count, gp, out, sem):
+        self.count, self.gp, self.out, self.sem = count, gp, out, sem
+
+    @classmethod
+    def scratch(cls, count):
+        return [pltpu.VMEM((cls.SLOTS, 4, 256, CW), bf), pltpu.SemaphoreType.DMA((count,))]
+
+    def slot(self, t):
+        return lax.rem(t, self.SLOTS)
+
+    def copy(self, t):
+        return pltpu.make_async_copy(self.gp.at[self.slot(t)], self.out.at[t], self.sem.at[t])
+
+    def tick(self, j, i):
+        if i == 0:
+            pl.when((j >= 0) & (j < self.count))(lambda: self.copy(j).start())
+
+    def release(self, t):
+        self.copy(t).wait()
+
+
+def reducer(comm, count, out, sizes, scratch):
+    if not comm:
+        return Keep(count, scratch[0], out, scratch[1])
+    at = Place()
+    at.barrier()
+    return Reduce(at, count, *scratch[:6], out, *scratch[6:], sizes)
+
+
+def put_chunk(red, j, m, left, right):
+    s, n = red.slot(j), left.shape[1]
+    for i in range(2):
+        red.gp[s, 2 * m + i, :, 0:n] = left[256 * i : 256 * (i + 1)].astype(bf)
+        red.gp[s, 2 * m + i, :, n:CW] = right[256 * i : 256 * (i + 1)].astype(bf)
+
+
+def f2_kernel(rows, comm, n2_h, g_h, mid_h, w_h, b_up, b_down, g2,
               out_h, gm_h, gb_h, gw_h, db_up, db_down, dg2, db2,
-              n2, g, n2t, gt, w, act, dhid, acc_o, acc_d, gp, mid, ob, gb, lsem, wsem, osem, msem):
+              n2, g, n2t, gt, w, act, dhid, acc_o, acc_d, mid, ob, gb, lsem, wsem, osem, msem, *scratch):
     KP = n2t.shape[1]
     NR = rows // PAIR
     first = QUADS
@@ -421,6 +587,7 @@
     c2 = pltpu.make_async_copy(g_h, g, lsem.at[1])
     c2.start()
     wcopy(0, 0).start()
+    red = reducer(comm, chunks, gw_h, w_h, scratch)
     n2t[:, rows:KP] = jnp.zeros((D, KP - rows), bf)
     gt[:, rows:KP] = jnp.zeros((D, KP - rows), bf)
     act[rows:KP, :] = jnp.zeros((KP - rows, FC), bf)
@@ -454,21 +621,27 @@
             acc_d[sl, :] += dot(dh, w[s, :, 0:FC], NT)
             return inner
 
-        lax.fori_loop(0, NR, block, 0)
+        red.tick(j - 1, 0)
+        for r in range(NR):
+            block(r, 0)
+            red.tick(j - 1, r + 1)
         db_up[pl.ds(j, 1), :] = dot(jnp.ones((8, KP), bf), dhid[...])[0:1]
 
-        @pl.when(j > 0)
+        @pl.when(j >= red.SLOTS)
         def _():
-            pltpu.make_async_copy(gp, gw_h.at[j - 1], osem.at[0]).wait()
+            red.release(j - red.SLOTS)
 
         def grads(m, inner):
             sl = pl.ds(pl.multiple_of(m * 512, 512), 512)
-            gp[sl, 0:FC] = dot(n2t[sl, :], dhid[...]).astype(bf)
-            gp[sl, FC:CW] = dot(gt[sl, :], act[...]).astype(bf)
+            put_chunk(red, j, m, dot(n2t[sl, :], dhid[...]), dot(gt[sl, :], act[...]))
+
+            @pl.when(m == 0)
+            def _():
+                red.tick(j - 1, 3)
+
             return inner
 
         lax.fori_loop(0, D // 512, grads, 0)
-        pltpu.make_async_copy(gp, gw_h.at[j], osem.at[0]).start()
         return carry
 
     lax.fori_loop(0, chunks, chunk, 0)
@@ -504,6 +677,7 @@
         dg2[...] += jnp.sum(dn * xhat, axis=0, keepdims=True)
         db2[...] += jnp.sum(dn, axis=0, keepdims=True)
         db_down[...] += jnp.sum(cot, axis=0, keepdims=True)
+        end_tick(red, chunks - 1, r)
         return carry
 
     lax.fori_loop(0, blocks, last, 0)
@@ -511,36 +685,49 @@
             pltpu.make_async_copy(gb, gb_h, osem.at[3])]
     for o in outs:
         o.start()
-    pltpu.make_async_copy(gp, gw_h.at[chunks - 1], osem.at[0]).wait()
+    finish(red, comm, blocks)
     for o in outs:
         o.wait()
 
 
-def f2(rows, n2, g, mid, w, b_up, b_down, g2):
+def end_tick(red, last, r):
+    for i in range(4):
+        pl.when(lax.rem(r, 4) == i)(functools.partial(red.tick, last + lax.div(r, 4), i))
+
+
+def finish(red, comm, done):
+    last = red.count - 1
+    if comm:
+        red.drain(last + done // 4, done % 4, last)
+    for t in range(max(0, red.count - red.SLOTS), red.count):
+        red.release(t)
+
+
+def f2(rows, comm, n2, g, mid, w, b_up, b_down, g2):
     A, V = any_spec(), vmem_spec()
     KP = -(-rows // 256) * 256
     chunks = w.shape[0] - QUADS
     RB = PAIR // 7
     return pl.pallas_call(
-        functools.partial(f2_kernel, rows),
-        out_shape=(sds((rows, D), bf), sds((rows, D), f32), sds((rows, D), bf), sds((chunks, D, CW), bf), sds((chunks, FC), f32),
+        functools.partial(f2_kernel, rows, comm),
+        out_shape=(sds((rows, D), bf), sds((rows, D), f32), sds((rows, D), bf), grad_shape(comm, chunks), sds((chunks, FC), f32),
                    sds((1, D), f32), sds((1, D), f32), sds((1, D), f32)),
         in_specs=[A, A, A, A, V, V, V],
         out_specs=(A, A, A, A, V, V, V, V),
         scratch_shapes=[
             pltpu.VMEM((rows, D), bf), pltpu.VMEM((rows, D), bf), pltpu.VMEM((D, KP), bf), pltpu.VMEM((D, KP), bf),
             pltpu.VMEM((2, D, CW), bf), pltpu.VMEM((KP, FC), bf), pltpu.VMEM((KP, FC), bf),
-            pltpu.VMEM((rows, D), f32), pltpu.VMEM((rows, D), f32), pltpu.VMEM((D, CW), bf),
+            pltpu.VMEM((rows, D), f32), pltpu.VMEM((rows, D), f32),
             pltpu.VMEM((2, RB, D), f32), pltpu.VMEM((rows, D), bf), pltpu.VMEM((rows, D), bf),
             pltpu.SemaphoreType.DMA((2,)), pltpu.SemaphoreType.DMA((2,)), pltpu.SemaphoreType.DMA((4,)),
             pltpu.SemaphoreType.DMA((2,)),
-        ],
-        compiler_params=pltpu.CompilerParams(vmem_limit_bytes=VMEM_LIMIT),
+        ] + (Reduce if comm else Keep).scratch(chunks),
+        compiler_params=kernel_params(comm, 1),
         name="feed_forward",
     )(n2, g, mid, w, b_up, b_down, g2)
 
 
-def attention_backward(pairs, mixed, datt, bias, lse, dmixed, dq, dk, dv, quad):
+def attention_backward(pairs, mixed, datt, bias, lse, dmixed, dq, dk, dv, quad, hook):
     def one(i, carry):
         p, hp = i // 2, lax.rem(i, 2)
         base = pl.multiple_of(p * PAIR, 16)
@@ -583,15 +770,16 @@
         dmixed[rows, pl.ds(lane0, 128)] = (dq[...] * SCALE).astype(bf)
         dmixed[rows, pl.ds(pl.multiple_of(lane0 + QW, 128), 128)] = dk[...].astype(bf)
         dmixed[rows, pl.ds(pl.multiple_of(lane0 + 2 * QW, 128), 128)] = dv[...].astype(bf)
+        hook(i)
         return carry
 
     lax.fori_loop(0, pairs * 2, one, 0)
 
 
-def f3_kernel(rows, gb_h, normed_h, w_h, mixed_h, att_h, lse, x_h, gm_h, g1, lab_col, lab_row, q_units, k_units,
+def f3_kernel(rows, comm, gb_h, normed_h, w_h, mixed_h, att_h, lse, x_h, gm_h, g1, lab_col, lab_row, q_units, k_units,
               gt_h, gw_h, db_qkv, db_out, dg1, db1,
-              gb, normed, gbt, normedt, w, mixed, att, datt, dmixed, bias, acc, dq, dk, dv, gp, xb, gmb, ob,
-              lsem, wsem, isem, osem, xsem, gsem, tsem):
+              gb, normed, gbt, normedt, w, mixed, att, datt, dmixed, bias, acc, dq, dk, dv, xb, gmb, ob,
+              lsem, wsem, isem, xsem, gsem, tsem, *scratch):
     KP = gbt.shape[1]
     pairs = rows // PAIR
 
@@ -606,6 +794,7 @@
     c2.start()
     for c in inputs(0, 0):
         c.start()
+    red = reducer(comm, QUADS, gw_h, w_h, scratch)
     gbt[:, rows:KP] = jnp.zeros((D, KP - rows), bf)
     normedt[:, rows:KP] = jnp.zeros((D, KP - rows), bf)
     dmixed[rows:KP, :] = jnp.zeros((KP - rows, 3 * QW), bf)
@@ -633,22 +822,31 @@
             datt[sl, :] = dot(gb[sl, :], w[s, :, 3 * QW : CW]).astype(bf)
             return inner
 
+        red.tick(k - 1, 0)
         lax.fori_loop(0, pairs, back, 0)
-        attention_backward(pairs, mixed.at[s], datt, bias, lse, dmixed, dq, dk, dv, k)
+
+        def hook(i):
+            pl.when(i == pairs - 1)(functools.partial(red.tick, k - 1, 1))
+            pl.when(i == 2 * pairs - 1)(functools.partial(red.tick, k - 1, 2))
+
+        attention_backward(pairs, mixed.at[s], datt, bias, lse, dmixed, dq, dk, dv, k, hook)
         db_qkv[pl.ds(k, 1), :] = dot(jnp.ones((8, KP), bf), dmixed[...])[0:1]
 
-        @pl.when(k > 0)
+        @pl.when(k >= red.SLOTS)
         def _():
-            pltpu.make_async_copy(gp, gw_h.at[k - 1], osem.at[0]).wait()
+            red.release(k - red.SLOTS)
 
         def grads(m, inner):
             sl = pl.ds(pl.multiple_of(m * 512, 512), 512)
-            gp[sl, 0 : 3 * QW] = dot(normedt[sl, :], dmixed[...]).astype(bf)
-            gp[sl, 3 * QW : CW] = dot(gbt[sl, :], att[s]).astype(bf)
+            put_chunk(red, k, m, dot(normedt[sl, :], dmixed[...]), dot(gbt[sl, :], att[s]))
+
+            @pl.when(m == 0)
+            def _():
+                red.tick(k - 1, 3)
+
             return inner
 
         lax.fori_loop(0, D // 512, grads, 0)
-        pltpu.make_async_copy(gp, gw_h.at[k], osem.at[0]).start()
 
         def back_in(r, inner):
             sl = pl.ds(pl.multiple_of(r * PAIR, 16), PAIR)
@@ -696,21 +894,22 @@
         pltpu.make_async_copy(ob.at[s], gt_h.at[part(r)], tsem.at[s]).start()
         dg1[...] += jnp.sum(dn * xhat, axis=0, keepdims=True)
         db1[...] += jnp.sum(dn, axis=0, keepdims=True)
+        end_tick(red, QUADS - 1, r)
         return carry
 
     lax.fori_loop(0, blocks, last, 0)
     for r in (blocks - 2, blocks - 1):
         pltpu.make_async_copy(ob.at[r % 2], gt_h.at[part(r)], tsem.at[r % 2]).wait()
-    pltpu.make_async_copy(gp, gw_h.at[QUADS - 1], osem.at[0]).wait()
-
-
-def f3(rows, gb, normed, w, mixed, att, lse, x, gm, g1, lab_col, lab_row, q_units, k_units):
+    finish(red, comm, blocks)
+
+
+def f3(rows, comm, gb, normed, w, mixed, att, lse, x, gm, g1, lab_col, lab_row, q_units, k_units):
     A, V = any_spec(), vmem_spec()
     KP = -(-rows // 256) * 256
     RB = PAIR // 7
     return pl.pallas_call(
-        functools.partial(f3_kernel, rows),
-        out_shape=(sds((rows, D), f32), sds((QUADS, D, CW), bf), sds((QUADS, 3 * QW), f32), sds((1, D), f32), sds((1, D), f32),
+        functools.partial(f3_kernel, rows, comm),
+        out_shape=(sds((rows, D), f32), grad_shape(comm, QUADS), sds((QUADS, 3 * QW), f32), sds((1, D), f32), sds((1, D), f32),
                    sds((1, D), f32)),
         in_specs=[A, A, A, A, A, V, A, A, V, V, V, V, V],
         out_specs=(A, A, V, V, V, V),
@@ -718,13 +917,12 @@
             pltpu.VMEM((rows, D), bf), pltpu.VMEM((rows, D), bf), pltpu.VMEM((D, KP), bf), pltpu.VMEM((D, KP), bf),
             pltpu.VMEM((2, D, CW), bf), pltpu.VMEM((2, rows, 3 * QW), bf), pltpu.VMEM((2, KP, QW), bf), pltpu.VMEM((rows, QW), bf),
             pltpu.VMEM((KP, 3 * QW), bf), pltpu.VMEM((rows // PAIR * 4, QMAX, KEYS), f32), pltpu.VMEM((rows, D), f32),
-            pltpu.VMEM((PAIR, 128), f32), pltpu.VMEM((PAIR, 128), f32), pltpu.VMEM((PAIR, 128), f32), pltpu.VMEM((D, CW), bf),
+            pltpu.VMEM((PAIR, 128), f32), pltpu.VMEM((PAIR, 128), f32), pltpu.VMEM((PAIR, 128), f32),
             pltpu.VMEM((2, RB, D), f32), pltpu.VMEM((2, RB, D), f32), pltpu.VMEM((2, RB, D), f32),
             pltpu.SemaphoreType.DMA((2,)), pltpu.SemaphoreType.DMA((2,)), pltpu.SemaphoreType.DMA((2, 2)),
-            pltpu.SemaphoreType.DMA((1,)), pltpu.SemaphoreType.DMA((2,)), pltpu.SemaphoreType.DMA((2,)),
-            pltpu.SemaphoreType.DMA((2,)),
-        ],
-        compiler_params=pltpu.CompilerParams(vmem_limit_bytes=VMEM_LIMIT),
+            pltpu.SemaphoreType.DMA((2,)), pltpu.SemaphoreType.DMA((2,)), pltpu.SemaphoreType.DMA((2,)),
+        ] + (Reduce if comm else Keep).scratch(QUADS),
+        compiler_params=kernel_params(comm, 2),
         name="attention_backward",
     )(gb, normed, w, mixed, att, lse, x, gm, g1, lab_col, lab_row, q_units, k_units)
 
@@ -803,14 +1001,16 @@
         up_bias = lax.all_gather(bias_up, "fsdp", axis=0, tiled=True).astype(f32).reshape(-1, FC)
         w = lax.all_gather(shard, "fsdp", axis=1, tiled=True)
         x, normed, mixed, att, lse, mid, n2, vec, b_up = f1(rows, False, chunks, tokens, ohy, ohx, tab, *lab, gathered, up_bias, w)
-    out, gm, gb, gw_ff, db_up, db_down, dg2, db2 = f2(rows, n2, grad_out, mid, w, b_up, vec[7:8], vec[5:6])
-    grad_tokens, gw_att, db_qkv, db_out, dg1, db1 = f3(rows, gb, normed, w, mixed, att, lse, x, gm, vec[0:1], *lab)
+    out, gm, gb, gw_ff, db_up, db_down, dg2, db2 = f2(rows, comm, n2, grad_out, mid, w, b_up, vec[7:8], vec[5:6])
+    grad_tokens, gw_att, db_qkv, db_out, dg1, db1 = f3(rows, comm, gb, normed, w, mixed, att, lse, x, gm, vec[0:1], *lab)
     small_grads = jnp.concatenate([dg1, db1, db_qkv[:, 0:QW].reshape(1, D), db_qkv[:, 2 * QW :].reshape(1, D), db_out, dg2, db2,
                                    db_down], axis=0)
     small_grads = jnp.concatenate([small_grads.reshape(8, fsdp, n).transpose(1, 0, 2).reshape(fsdp, 8 * n),
                                    db_up.reshape(fsdp, 4 * n)], axis=1)
     gw = jnp.concatenate([gw_att, gw_ff], axis=0)
-    gw = lax.psum(lax.psum_scatter(gw, "fsdp", scatter_dimension=1, tiled=True), "dp").astype(f32)
+    if not comm:
+        gw = lax.psum(lax.psum_scatter(gw.reshape(chunks, D, CW), "fsdp", scatter_dimension=1, tiled=True), "dp")
+    gw = gw.astype(f32)
     sg = lax.psum(lax.psum_scatter(small_grads, "fsdp", scatter_dimension=0, tiled=True), "dp").reshape(12, n)
     g_att, g_ff = gw[:QUADS], gw[QUADS:]
     g_qkv = g_att[:, :, : 3 * QW].reshape(QUADS, n, 3, QW).transpose(1, 2, 0, 3).reshape(n, 3 * D)

time: 859 us -> 584 us (0.68)
  waiting for transfers between devices: 295 us -> 0 us
  Pallas kernels: 443 us -> 489 us
  other arithmetic: 29.1 us -> 7.4 us
  between operations: 15 us -> 1.64 us
  local copies, waits for them, and re-layouts: 29.4 us -> 40.3 us
    reduce_scatter x1 -> x0, waiting for transfers between devices: 245 us -> none  [local(): lax.psum_scatter(gw, 'fsdp', scatter_dimension=1, tiled=True)]
    psum x1 -> x0, waiting for transfers between devices: 49.5 us -> none  [local(): lax.psum(lax.psum_scatter(gw, 'fsdp', scatter_dimension=1, tiled=True), '...]
    pallas_call x2, Pallas kernels: 251 us -> 296 us  [the longest x1 152 us: f3(): pl.pallas_call(functools.partial(f3_kernel, rows, comm), out_shape=(sds((...]
    concatenate x1 -> x0, other arithmetic: 21 us -> none  [local(): gw = jnp.concatenate([gw_att, gw_ff], axis=0)]
    unnamed x53 -> x63, local copies, waits for them, and re-layouts: 7.95 us -> 19.7 us
  transfers between devices with their start and end apart: 2 -> 0, of which waited for: 2 -> 0; matrix products, arithmetic and copies ran while one was open for 0% -> 0% of each run, Pallas kernels for 0% -> 0%
where the time goes in v2:
time: 584 us; the launch traced here: 573 us
  Pallas kernels  489 us (84%)
  local copies, waits for them, and re-layouts  40.3 us (7%)
  blocking collectives  35.4 us (6%)
  other arithmetic  7.4 us (1%)
    pallas_call x1, Pallas kernels, f1(): pl.pallas_call(functools.partial(f1_kernel, rows, comm), out_shape=out_sh...  193 us
    pallas_call x1, Pallas kernels, f3(): pl.pallas_call(functools.partial(f3_kernel, rows, comm), out_shape=(sds((...  152 us
    pallas_call x1, Pallas kernels, f2(): pl.pallas_call(functools.partial(f2_kernel, rows, comm), out_shape=(sds((...  144 us
    unnamed x1, blocking collectives  26.3 us
    unnamed x63, local copies, waits for them, and re-layouts  19.7 us

profile of v2, /device:TPU:0, one launch (start us, length us, event | category | flops | bytes accessed | tf_op | source)
XLA Modules:
  0.0 573.5 jit_solution(3003231353129862245)
XLA Ops:
  1.6 0.9 multiply_sine_fusion
  2.6 1.0 pad_maximum_fusion.refs_3_
  5.9 1.7 copy.72
  8.1 1.5 copy.74
  9.9 1.9 maximum_maximum_fusion.refs_9_
  11.9 1.2 concatenate.42.refs_8_
  13.1 192.8 %attention_forward.1 = (f32[1568,1024]{1,0:T(8,128)}, bf16[1568,1024]{1,0:T(8,128)(2,1)}, bf16[4,1568,768]{2,1,0:T(8,128)(2,1)}, bf16[4,1568,256]{2,1,0:T(8,128)...) custom-call(bf16[1568,1024]{1,0:T(8,128)(2,1)} %refs_0_.1, ...), custom_call_target="tpu_custom_call" | custom-call | tf_op jit(solution)/shard_map/attention_forward/pallas_call | solution.py:410
  205.9 1.5 fusion.4
  207.4 144.4 %feed_forward.1 = (bf16[1568,1024]{1,0:T(8,128)(2,1)}, f32[1568,1024]{1,0:T(8,128)}, bf16[1568,1024]{1,0:T(8,128)(2,1)}, bf16[8,128,1024]{2,1,0:T(8,128)(2,1)}, ...) custom-call(bf16[1568,1024]{1,0:T(8,128)(2,1)} %get-tuple-element.39.n2_h, ...), custom_call_target="tpu_custom_call" | custom-call | tf_op jit(solution)/shard_map/feed_forward/pallas_call | solution.py:711
  351.8 151.6 %attention_backward.1 = (f32[1568,1024]{1,0:T(8,128)}, bf16[4,128,1024]{2,1,0:T(8,128)(2,1)}, f32[4,768]{1,0:T(4,128)}, f32[1,1024]{1,0:T(1,128)}, f32[1,1024]{1,0:T(1,128)}, /*index=5*/f32[1,1024]{1,0:T(1,128)}) custom-call(bf16[1568,1024]{1,0:T(8,128)(2,1)} %get-tuple-element.45.gb_h, bf16[1568,1024]{1,0:T(8,128)(2,1)} %get-tuple-element.46.normed_h, ...), custom_call_target="tpu_custom_call" | custom-call | tf_op jit(solution)/shard_map/attention_backward/pallas_call | solution.py:910
  503.3 1.6 maximum_convert_fusion
  505.0 2.8 slice_bitcast_fusion
  507.8 1.2 copy-done
  508.9 3.0 copy.80
  511.9 2.9 copy.83
  514.8 0.8 convert_bitcast_fusion
  515.6 2.0 copy.79
  517.7 2.9 copy.81
  520.6 1.5 slice.89
  522.8 1.6 copy.82
  524.6 26.3 %all-reduce.1 = f32[8,1536]{1,0:T(8,128)S(1)} all-reduce(f32[8,1536]{1,0:T(8,128)S(1)} %pad_maximum_fusion.1), channel_id=2, replica_groups=mesh['dp'=4,'fsdp'=8] {'fsdp'}, use_global_device_ids=true, to_apply=%region_1.2.clone | all-reduce | flops 12288 | bytes 98304
  552.1 9.1 %psum.7 = f32[1,1536]{1,0:T(1,128)S(1)} all-reduce(f32[1,1536]{1,0:T(1,128)S(1)} %constant_dynamic-slice_fusion), channel_id=1, replica_groups=mesh['dp'=4,'fsdp'=8] {'dp'}, use_global_device_ids=true, to_apply=%region_2.3 | all-reduce | flops 1536 | bytes 12288 | tf_op jit(solution)/shard_map/psum | solution.py:1014
  562.4 3.9 copy.93
  566.3 6.7 %copy.94 = f32[1568,1024]{1,0:T(8,128)} copy(f32[1568,1024]{1,0:T(8,128)} %get-tuple-element.144) | data formatting | bytes 12845056
  (83 shorter events, 7.1 us)
Async XLA Ops:
  0.6 2.9 copy-start.22
  0.7 4.5 copy-start.3
  5.9 3.7 copy-start.4
  9.8 2.0 copy-start.13
  9.8 2.0 copy-start.14
  9.8 2.0 copy-start.15
  9.8 2.0 copy-start.16
  9.8 2.0 copy-start.17
  9.9 2.0 copy-start.18
  9.9 2.0 copy-start.19
  9.9 2.0 copy-start.20
  9.9 2.0 copy-start.21
  351.8 151.6 %copy-start.1 = (bf16[8,128,1024]{2,1,0:T(8,128)(2,1)S(1)}, bf16[8,128,1024]{2,1,0:T(8,128)(2,1)}, u32[]{:S(2)}) copy-start(bf16[8,128,1024]{2,1,0:T(8,128)(2,1)} %get-tuple-element.62) | copy-start | bytes 6291460
  505.0 4.0 copy-start
  508.9 5.9 %copy-start.2 = (bf16[4,128,1024]{2,1,0:T(8,128)(2,1)S(1)}, bf16[4,128,1024]{2,1,0:T(8,128)(2,1)}, u32[]{:S(2)}) copy-start(bf16[4,128,1024]{2,1,0:T(8,128)(2,1)} %get-tuple-element.61) | copy-start | bytes 3145732
  522.6 1.8 copy-start.12
  522.6 1.8 copy-start.11
  522.6 1.8 copy-start.6
  522.6 1.9 copy-start.10
  522.6 1.9 copy-start.9
  522.6 1.9 copy-start.8
  522.6 1.9 copy-start.7
  522.6 1.9 copy-start.5
  522.6 28.2 %copy-start.23 = (u32[32]{0:T(128)S(1)}, u32[32]{0:T(128)}, u32[]{:S(2)}) copy-start(u32[32]{0:T(128)} %constant.40) | copy-start | bytes 388
